TPU v7x, 32 devices: a whole 2x2x4 slice. The times are simulated.
32 devices in a mesh: groups: 2 (over y), lon: 4 (over x, core), lat: 4 (over z).
Axes of the slice: x: 2, y: 2, z: 4, core: 2. Of those that a mesh axis runs over, the one named last changes fastest.
Arguments:
- heat_anomaly: float32 [16, 1024, 512], P('groups', 'lat', 'lon'), parts along dimension 0, may hold values from -6 to 6
- zonal_speed: float32 [16, 1024, 512], P('groups', 'lat', 'lon'), parts along dimension 0, may hold values from -18 to 18
- meridional_speed: float32 [16, 1024, 512], P('groups', 'lat', 'lon'), parts along dimension 0, may hold values from -18 to 18
- submerged_tiers_per_site: int32 [2048, 512], P(('groups', 'lat'), 'lon'), parts along dimension 0, may hold values from 0 to 8, as said below
Outputs:
- heat_anomaly_next: float32 [16, 1024, 512], P('groups', 'lat', 'lon'), parts along dimension 0
- zonal_speed_next: float32 [16, 1024, 512], P('groups', 'lat', 'lon'), parts along dimension 0
- meridional_speed_next: float32 [16, 1024, 512], P('groups', 'lat', 'lon'), parts along dimension 0
- free_height_anomaly: float32 [2048, 512], P(('groups', 'lat'), 'lon'), parts along dimension 0
There are 2 independent parts, one for each index of `groups`. A program takes and returns all parts, laid end to end along the dimension named above; each array names one. Nothing has to cross between parts.
Inputs may be any that keep to these rules, and one draw needn't show every extreme that they name: `submerged_tiers_per_site`: blocks of 8 x 128 cells tile the grid from row 0 and column 0; every cell of a land block is 0, the first cell of an ocean block is 1 or more; each band of 256 rows that starts at a multiple of 256 holds exactly 96 ocean blocks.
All inputs are finite; a program needn't handle non-finite values.
Results may differ from a plain program's by a relative error of at most 0.00015.
Values sent between devices are 32-bit elements; how exact they have to be, the bound alone decides.
A program may use at most 64 MiB of HBM per device.

v0:
```python
import jax
import jax.numpy as jnp
from jax import lax
from jax.sharding import PartitionSpec as P

BY = 8
ITERS = 4


TIME_STEP = 0.05
DIFFUSIVITY = 0.2
VISCOSITY = 0.2
HEAT_DILATION = 0.5
SURFACE_TERM = 0.01
ROW_DECAY = 0.6
COLUMN_DECAY = 0.6


def padded_2(array, sides, width):
    for axis, dim in sides:
        devices, length = (lax.axis_size(axis), array.shape[dim])
        up = [(i, (i + 1) % devices) for i in range(devices)]
        down = [(j, i) for i, j in up]
        last = lax.slice_in_dim(array, length - width, length, axis=dim)
        leading = lax.slice_in_dim(array, 0, width, axis=dim)
        before = lax.ppermute(last, axis, up)
        after = lax.ppermute(leading, axis, down)
        array = jnp.concatenate([before, array, after], axis=dim)
    return array


def layer_thickness(tier_number):
    position = jnp.arange(tier_number).astype(jnp.float32)
    return (position + 1.0) * (2.0 / (tier_number * (tier_number + 1)))


def decay_matrix(extent, decay_rate):
    position = jnp.arange(extent)
    distance = jnp.abs(position[:, None] - position[None, :]).astype(jnp.float32)
    return decay_rate**distance


def block_kernel(blocks, across_rows, across_cols):
    inner = jnp.einsum("ij,bjk->bik", across_rows, blocks, precision=lax.Precision.HIGHEST)
    return jnp.einsum("bik,kl->bil", inner, across_cols, precision=lax.Precision.HIGHEST)


def vertical_shear_part(
    heat_anomaly,
    zonal_current,
    meridional_current,
    marine_indicator,
    rotation_parameter,
    tier_floor,
    basin_pieces,
):
    weight_load = -HEAT_DILATION * jnp.cumsum(tier_floor[:, None, None] * heat_anomaly, axis=0)
    wet_mid, wet_east, wet_west, wet_north, wet_south = basin_pieces(marine_indicator)
    face_east = wet_mid * wet_east
    face_west = wet_mid * wet_west
    face_north = wet_mid * wet_north
    face_south = wet_mid * wet_south
    scalar_middle, scalar_right, scalar_left, scalar_upper, scalar_lower = basin_pieces(
        heat_anomaly
    )
    zonal_mid, zonal_east, zonal_west, zonal_north, zonal_south = basin_pieces(zonal_current)
    meridional_mid, meridional_east, meridional_west, meridional_north, meridional_south = (
        basin_pieces(meridional_current)
    )
    pressure_mid, pressure_east, pressure_west, pressure_north, pressure_south = basin_pieces(
        weight_load
    )
    diffusion = DIFFUSIVITY * (
        face_east * (scalar_right - scalar_middle)
        + face_west * (scalar_left - scalar_middle)
        + face_north * (scalar_upper - scalar_middle)
        + face_south * (scalar_lower - scalar_middle)
    )
    advection = 0.25 * (
        face_east * (zonal_mid + zonal_east) * (scalar_middle + scalar_right)
        - face_west * (zonal_mid + zonal_west) * (scalar_middle + scalar_left)
        + face_north * (meridional_mid + meridional_north) * (scalar_middle + scalar_upper)
        - face_south * (meridional_mid + meridional_south) * (scalar_middle + scalar_lower)
    )
    tracer_next = wet_mid * (scalar_middle + TIME_STEP * (diffusion - advection))
    slope_x = 0.5 * (
        face_east * (pressure_east - pressure_mid) + face_west * (pressure_mid - pressure_west)
    )
    slope_y = 0.5 * (
        face_north * (pressure_north - pressure_mid) + face_south * (pressure_mid - pressure_south)
    )
    spread_zonal = (
        face_east * (zonal_east - zonal_mid)
        + face_west * (zonal_west - zonal_mid)
        + face_north * (zonal_north - zonal_mid)
        + face_south * (zonal_south - zonal_mid)
    )
    spread_meridional = (
        face_east * (meridional_east - meridional_mid)
        + face_west * (meridional_west - meridional_mid)
        + face_north * (meridional_north - meridional_mid)
        + face_south * (meridional_south - meridional_mid)
    )
    zonal_speed_next = wet_mid * (
        zonal_mid
        + TIME_STEP * (rotation_parameter * meridional_mid - slope_x + VISCOSITY * spread_zonal)
    )
    meridional_speed_next = wet_mid * (
        meridional_mid
        + TIME_STEP * (-rotation_parameter * zonal_mid - slope_y + VISCOSITY * spread_meridional)
    )
    return (tracer_next, zonal_speed_next, meridional_speed_next)


def barotropic_forcing(wet_mid, transport_x, transport_y):
    return -wet_mid * 0.5 * (transport_x[1] - transport_x[2] + (transport_y[3] - transport_y[4]))


def surface_coefficients(wet_pieces, depth_pieces):
    wet_mid, wet_east, wet_west, wet_north, wet_south = wet_pieces
    depth_mid, depth_east, depth_west, depth_north, depth_south = depth_pieces
    link_east = wet_mid * wet_east * 0.5 * (depth_mid + depth_east)
    link_west = wet_mid * wet_west * 0.5 * (depth_mid + depth_west)
    link_north = wet_mid * wet_north * 0.5 * (depth_mid + depth_north)
    link_south = wet_mid * wet_south * 0.5 * (depth_mid + depth_south)
    diagonal = SURFACE_TERM + link_east + link_west + link_north + link_south
    return (diagonal, (link_east, link_west, link_north, link_south))


def apply_surface(quantity, neighbours, wet_mid, diagonal, links):
    return wet_mid * (
        diagonal * quantity
        - (
            links[0] * neighbours[0]
            + links[1] * neighbours[1]
            + links[2] * neighbours[2]
            + links[3] * neighbours[3]
        )
    )


def basin_pieces(values):
    return (
        values[..., 1:-1, 1:-1],
        values[..., 1:-1, 2:],
        values[..., 1:-1, :-2],
        values[..., 2:, 1:-1],
        values[..., :-2, 1:-1],
    )


def residual_product(residual, conditioned):
    return lax.psum(jnp.sum(residual * conditioned), ("lon", "lat"))


def local(heat_anomaly, zonal_speed, meridional_speed, submerged_tiers_per_site):
    tier_number, meridian_total, parallel_total = heat_anomaly.shape
    lat_devices = lax.axis_size("lat")
    lat_at = lax.axis_index("lat")
    total_rows = meridian_total * lat_devices
    tier_floor = layer_thickness(tier_number)
    marine_indicator = (
        lax.broadcasted_iota(jnp.int32, heat_anomaly.shape, 0) < submerged_tiers_per_site[None]
    ).astype(jnp.float32)
    joined_arrays = jnp.stack([heat_anomaly, zonal_speed, meridional_speed, marine_indicator])
    cycle_rows = lat_at * meridian_total - 1 + jnp.arange(meridian_total + 2)
    surface_valid = ((cycle_rows >= 0) & (cycle_rows < total_rows)).astype(jnp.float32)
    extended = padded_2(joined_arrays, (("lon", 3), ("lat", 2)), 2)
    wide_rows = lat_at * meridian_total - 2 + jnp.arange(meridian_total + 4)
    wide_valid = ((wide_rows >= 0) & (wide_rows < total_rows)).astype(jnp.float32)
    extended = extended * wide_valid[None, None, :, None]
    rotation_parameter = (2.0 * (cycle_rows.astype(jnp.float32) + 0.5) / total_rows - 1.0)[:, None]
    scalar_shifted, zonal_cycle, meridional_cycle = vertical_shear_part(
        extended[0],
        extended[1],
        extended[2],
        extended[3],
        rotation_parameter,
        tier_floor,
        basin_pieces,
    )
    heat_anomaly_next = scalar_shifted[:, 1:-1, 1:-1]
    zonal_speed_next = zonal_cycle[:, 1:-1, 1:-1]
    meridional_speed_next = meridional_cycle[:, 1:-1, 1:-1]
    transport_cycle_x = jnp.sum(tier_floor[:, None, None] * zonal_cycle, axis=0)
    transport_cycle_y = jnp.sum(tier_floor[:, None, None] * meridional_cycle, axis=0)
    wet_cycle = extended[3][:, 1:-1, 1:-1]
    depth_cycle = jnp.sum(tier_floor[:, None, None] * wet_cycle, axis=0)
    surface_wet_cycle = wet_cycle[0]
    wet_pieces = basin_pieces(surface_wet_cycle)
    wet_mid = wet_pieces[0]
    forcing = barotropic_forcing(
        wet_mid, basin_pieces(transport_cycle_x), basin_pieces(transport_cycle_y)
    )
    diagonal, links = surface_coefficients(wet_pieces, basin_pieces(depth_cycle))
    inverse_root = 1.0 / jnp.sqrt(diagonal)
    across_rows = decay_matrix(BY, ROW_DECAY)
    across_cols = decay_matrix(parallel_total, COLUMN_DECAY)
    block_count = meridian_total // BY

    def condition(quantity):
        scaled = (wet_mid * inverse_root * quantity).reshape(block_count, BY, parallel_total)
        result = block_kernel(scaled, across_rows, across_cols)
        return wet_mid * inverse_root * result.reshape(meridian_total, parallel_total)

    free_height_anomaly = jnp.zeros((meridian_total, parallel_total), jnp.float32)
    residual = forcing
    conditioned = condition(residual)
    direction = conditioned
    progress = residual_product(residual, conditioned)
    for iteration in range(ITERS):
        padded = padded_2(direction, (("lon", 1), ("lat", 0)), 1)
        padded = padded * surface_valid[:, None]
        applied = apply_surface(direction, basin_pieces(padded)[1:], wet_mid, diagonal, links)
        step_size = progress / lax.psum(jnp.sum(direction * applied), ("lon", "lat"))
        free_height_anomaly = free_height_anomaly + step_size * direction
        residual = residual - step_size * applied
        if iteration + 1 < ITERS:
            conditioned = condition(residual)
            following = residual_product(residual, conditioned)
            direction = conditioned + following / progress * direction
            progress = following
    return (heat_anomaly_next, zonal_speed_next, meridional_speed_next, free_height_anomaly)


def solution(mesh):
    placed = (
        P("groups", "lat", "lon"),
        P("groups", "lat", "lon"),
        P("groups", "lat", "lon"),
        P(("groups", "lat"), "lon"),
    )
    return jax.shard_map(
        local,
        mesh=mesh,
        in_specs=placed,
        out_specs=(
            P("groups", "lat", "lon"),
            P("groups", "lat", "lon"),
            P("groups", "lat", "lon"),
            P(("groups", "lat"), "lon"),
        ),
        check_vma=False,
    )
```

profile of v0, /device:TPU:0, one launch (start us, length us, event | category | flops | bytes accessed | tf_op | source)
XLA Modules:
  0.0 385.4 jit_solution(3603984679115259660)
XLA Ops:
  0.6 1.0 fusion.43
  1.6 2.1 pad_maximum_fusion
  3.8 4.7 %fusion.126 = (f32[4,8,256,2]{3,2,1,0:T(8,128)}, f32[4,8,256,2]{3,2,1,0:T(8,128)}) fusion(f32[4,8,256,128]{3,2,1,0:T(8,128)S(1)} %pad_maximum_fusion), kind=kLoop, calls=%fused_computation.224 | loop fusion | bytes 262144 | tf_op jit(solution)/shard_map/slice | solution.py:24
  8.5 2.8 copy.21
  11.3 2.4 collective-permute-start.1
  13.7 2.8 copy.20
  16.7 3.6 collective-permute-done
  20.3 2.6 copy.22
  23.0 2.6 copy.23
  25.6 1.5 pad_maximum_fusion.6
  27.1 1.6 collective-permute-start.2
  28.8 2.2 collective-permute-start.3
  31.0 2.3 collective-permute-done.2
  33.4 0.4 collective-permute-done.3
  33.7 7.6 %maximum_multiply_fusion = f32[4,8,260,132]{3,2,1,0:T(8,128)S(1)} fusion(f32[4,8,2,132]{3,2,1,0:T(2,128)S(1)} %collective-permute-done.3, f32[4,8,256,2]{3,2,1,0:T(8,128)S(1)} %copy-done.3, f32[1,8,256,128]{3,2,1,0:T(8,128)S(1)} %fusion.43, f32[1,8,256,128]{3,2,1,0:T(8,128)S(1)} %bitcast.82, f32[1,8,256,128]{3,2,1,0:T(8,128)S(1)} %bitcast.85, ...), kind=kLoop, calls=%fused_computation | loop fusion | flops 8785920 | bytes 8786960 | tf_op jit(solution)/shard_map/mul | solution.py:171
  41.3 1.9 slice_bitcast_fusion.1
  43.3 1.8 fusion.31
  45.1 1.0 slice_bitcast_fusion.4
  46.1 14.4 %multiply_reduce_fusion.2 = (f32[258,130]{1,0:T(8,128)}, f32[258,130]{1,0:T(8,128)}, f32[258,130]{1,0:T(8,128)}, f32[8,258,130]{2,1,0:T(8,128)}, f32[8,258,130]{2,1,0:T(8,128)}) fusion(f32[8]{0:T(128)S(1)} %add_multiply_fusion.1, f32[8,260,132]{2,1,0:T(8,128)S(1)} %get-tuple-element.32, f32[8,260,132]{2,1,0:T(8,128)S(1)} %get-tuple-element.30, ...), kind=kLoop, calls=%fused_computation.49 | loop fusion | flops 15461940 | bytes 24016736 | tf_op jit(solution)/shard_map/reduce_sum | solution.py:185
  60.4 2.8 rsqrt_multiply_fusion
  64.0 1.7 collective-permute-start.5
  65.7 3.1 collective-permute-done.4
  68.9 0.6 collective-permute-start.6
  69.5 3.2 collective-permute-start.7
  72.7 1.5 collective-permute-done.6
  74.5 1.5 multiply_reduce_fusion.8
  76.0 33.4 %all-reduce = (f32[]{:T(128)}, f32[]{:T(128)}) all-reduce(f32[]{:T(128)} %get-tuple-element.9, f32[]{:T(128)} %get-tuple-element.8), channel_id=1, replica_groups=mesh['groups'=2,'lon'=4,'lat'=4] {'lon','lat'}, use_global_device_ids=true, to_apply=%region_5.6 | all-reduce | flops 2 | bytes 16 | tf_op jit(solution)/shard_map/psum | solution.py:153
  110.7 0.9 multiply_subtract_fusion.2
  112.0 1.5 multiply_reduce_fusion.7
  113.5 30.3 %psum.58 = f32[]{:T(128)} all-reduce(f32[]{:T(128)} %get-tuple-element.58), channel_id=1, replica_groups=mesh['groups'=2,'lon'=4,'lat'=4] {'lon','lat'}, use_global_device_ids=true, to_apply=%region_9.10 | all-reduce | flops 1 | bytes 8 | tf_op jit(solution)/shard_map/psum | solution.py:153
  145.2 0.9 multiply_add_fusion.5
  146.3 1.7 collective-permute-start.9
  148.0 2.7 collective-permute-done.8
  150.7 2.3 collective-permute-start.10
  153.0 1.5 collective-permute-start.11
  154.6 1.5 collective-permute-done.10
  156.1 0.5 collective-permute-done.11
  156.8 1.5 multiply_reduce_fusion.6
  158.3 33.5 %psum.59 = f32[]{:T(128)} all-reduce(f32[]{:T(128)} %get-tuple-element.17), channel_id=1, replica_groups=mesh['groups'=2,'lon'=4,'lat'=4] {'lon','lat'}, use_global_device_ids=true, to_apply=%region_11.12 | all-reduce | flops 1 | bytes 8 | tf_op jit(solution)/shard_map/psum | solution.py:215
  193.1 1.0 multiply_subtract_fusion.1
  194.4 1.5 multiply_reduce_fusion.5
  195.9 30.3 %psum.60 = f32[]{:T(128)} all-reduce(f32[]{:T(128)} %get-tuple-element.60), channel_id=1, replica_groups=mesh['groups'=2,'lon'=4,'lat'=4] {'lon','lat'}, use_global_device_ids=true, to_apply=%region_13.14 | all-reduce | flops 1 | bytes 8 | tf_op jit(solution)/shard_map/psum | solution.py:153
  227.5 0.9 multiply_add_fusion.4
  228.6 1.7 collective-permute-start.13
  230.4 2.7 collective-permute-done.12
  233.2 2.2 collective-permute-start.14
  235.4 1.6 collective-permute-start.15
  237.0 17.2 %multiply_add_fusion = (f32[8,258,130]{2,1,0:T(8,128)}, f32[8,258,130]{2,1,0:T(8,128)}) fusion(f32[8,260,132]{2,1,0:T(8,128)} %copy-done.1, f32[8,260,132]{2,1,0:T(8,128)} %copy-done, f32[8,260,132]{2,1,0:T(8,128)} %get-tuple-element.31, f32[8,260,132]{2,1,0:T(8,128)S(1)} %get-tuple-element.32), kind=kLoop, calls=%fused_computation.53 | loop fusion | flops 5903040 | bytes 19319040 | tf_op jit(solution)/shard_map/add | solution.py:80
  254.4 1.5 multiply_reduce_fusion.4
  255.9 31.2 %psum.61 = f32[]{:T(128)} all-reduce(f32[]{:T(128)} %get-tuple-element.15), channel_id=1, replica_groups=mesh['groups'=2,'lon'=4,'lat'=4] {'lon','lat'}, use_global_device_ids=true, to_apply=%region_15.16 | all-reduce | flops 1 | bytes 8 | tf_op jit(solution)/shard_map/psum | solution.py:215
  288.4 1.2 convolution_bitcast_fusion.1
  289.6 2.4 multiply_reduce_fusion.3
  292.0 31.7 %psum.62 = f32[]{:T(128)} all-reduce(f32[]{:T(128)} %get-tuple-element.62), channel_id=1, replica_groups=mesh['groups'=2,'lon'=4,'lat'=4] {'lon','lat'}, use_global_device_ids=true, to_apply=%region_17.18 | all-reduce | flops 1 | bytes 8 | tf_op jit(solution)/shard_map/psum | solution.py:153
  325.1 0.9 multiply_add_fusion.3
  326.2 1.7 collective-permute-start.17
  327.9 9.3 %multiply_add_fusion.1 = (f32[8,258,130]{2,1,0:T(8,128)S(1)}, f32[8,258,130]{2,1,0:T(8,128)S(1)}, f32[8,258,130]{2,1,0:T(8,128)S(1)}, f32[8,258,130]{2,1,0:T(8,128)S(1)}) fusion(f32[8,260,132]{2,1,0:T(8,128)} %get-tuple-element.31, f32[8,260,132]{2,1,0:T(8,128)S(1)} %get-tuple-element.32), kind=kLoop, calls=%fused_computation.55 | loop fusion | flops 3756480 | bytes 15025920 | tf_op jit(solution)/shard_map/add | solution.py:74
  337.3 1.0 collective-permute-start.18
  338.3 2.9 collective-permute-start.19
  341.1 4.9 %slice_multiply_fusion.4 = f32[8,256,128]{2,1,0:T(8,128)} fusion(f32[8,258,130]{2,1,0:T(8,128)S(1)} %get-tuple-element.39, f32[8,258,130]{2,1,0:T(8,128)S(1)} %get-tuple-element.40, f32[8,258,130]{2,1,0:T(8,128)} %get-tuple-element.34, f32[8,258,130]{2,1,0:T(8,128)} %get-tuple-element.33, f32[8,258,130]{2,1,0:T(8,128)S(1)} %get-tuple-element.36, ...), kind=kLoop, calls=%fused_computation.70 | loop fusion | flops 2097152 | bytes 7340032 | tf_op jit(solution)/shard_map/mul | solution.py:85
  346.1 3.0 slice.373
  349.3 0.8 fusion.48
  350.1 2.9 slice.368
  353.0 30.4 %psum.63 = f32[]{:T(128)} all-reduce(f32[]{:T(128)} %fusion.48), channel_id=1, replica_groups=mesh['groups'=2,'lon'=4,'lat'=4] {'lon','lat'}, use_global_device_ids=true, to_apply=%region_19.20 | all-reduce | flops 1 | bytes 8 | tf_op jit(solution)/shard_map/psum | solution.py:215
  384.7 0.7 multiply_add_fusion.2
  (60 shorter events, 2.9 us)
Async XLA Ops:
  11.3 11.6 %collective-permute-start.1 = (f32[4,8,256,2]{2,1,3,0:T(8,128)S(1)}, f32[4,8,256,2]{2,1,3,0:T(8,128)S(1)}, u32[]{:S(2)}, u32[]{:S(2)}) collective-permute-start(f32[4,8,256,2]{2,1,3,0:T(8,128)S(1)} %copy.21), channel_id=1, source_target_pairs={{4,0},{8,4},{12,8},{0,12},{5,1},{9,5},{13,9},{1,13},{6,2},{10,6},{... | collective-permute-start | bytes 196616 | tf_op jit(solution)/shard_map/ppermute | solution.py:27
  16.6 3.7 collective-permute-start
  23.0 2.6 copy-start.4
  23.0 2.6 copy-start.5
  25.6 8.2 %copy-start.2 = (f32[4,8,256,2]{3,2,1,0:T(8,128)S(1)}, f32[4,8,256,2]{3,2,1,0:T(8,128)}, u32[]{:S(2)}) copy-start(f32[4,8,256,2]{3,2,1,0:T(8,128)} %copy.22) | copy-start | bytes 196612
  25.6 8.2 %copy-start.3 = (f32[4,8,256,2]{3,2,1,0:T(8,128)S(1)}, f32[4,8,256,2]{3,2,1,0:T(8,128)}, u32[]{:S(2)}) copy-start(f32[4,8,256,2]{3,2,1,0:T(8,128)} %copy.23) | copy-start | bytes 196612
  25.6 8.1 %copy-start.6 = (f32[8,256,128]{2,1,0:T(8,128)S(1)}, f32[8,256,128]{2,1,0:T(8,128)}, u32[]{:S(2)}) copy-start(f32[8,256,128]{2,1,0:T(8,128)} %param.4) | copy-start | bytes 3145732
  27.1 6.2 %collective-permute-start.2 = (f32[4,8,2,132]{3,2,1,0:T(2,128)S(1)}, f32[4,8,2,132]{3,2,1,0:T(2,128)S(1)}, u32[]{:S(2)}, u32[]{:S(2)}) collective-permute-start(f32[4,8,2,132]{3,2,1,0:T(2,128)S(1)} %get-tuple-element.27), channel_id=1, source_target_pairs={{0,1},{1,2},{2,3},{3,0},{4,5},{5,6},{6,7},{7,4},{8,9},{9,10},{10,1... | collective-permute-start | bytes 101384 | tf_op jit(solution)/shard_map/ppermute | solution.py:26
  28.8 5.0 %collective-permute-start.3 = (f32[4,8,2,132]{3,2,1,0:T(2,128)S(1)}, f32[4,8,2,132]{3,2,1,0:T(2,128)S(1)}, u32[]{:S(2)}, u32[]{:S(2)}) collective-permute-start(f32[4,8,2,132]{3,2,1,0:T(2,128)S(1)} %get-tuple-element.28), channel_id=1, source_target_pairs={{1,0},{2,1},{3,2},{0,3},{5,4},{6,5},{7,6},{4,7},{9,8},{10,9},{11,1... | collective-permute-start | bytes 101384 | tf_op jit(solution)/shard_map/ppermute | solution.py:27
  43.3 2.8 copy-start
  43.3 2.8 copy-start.1
  60.4 14.0 %copy-start.7 = (f32[258,130]{1,0:T(8,128)S(1)}, f32[258,130]{1,0:T(8,128)}, u32[]{:S(2)}) copy-start(f32[258,130]{1,0:T(8,128)} %slice_bitcast_fusion.4) | copy-start | bytes 402484
  63.3 93.5 %copy-start.8 = (f32[256,128]{1,0:T(8,128)}, f32[256,128]{1,0:T(8,128)S(1)}, u32[]{:S(2)}) copy-start(f32[256,128]{1,0:T(8,128)S(1)} %get-tuple-element.24) | copy-start | bytes 393220
  63.9 4.9 %collective-permute-start.4 = (f32[256,1]{1,0:T(8,128)S(1)}, f32[256,1]{1,0:T(8,128)S(1)}, u32[]{:S(2)}, u32[]{:S(2)}) collective-permute-start(f32[256,1]{1,0:T(8,128)S(1)} %get-tuple-element.56), channel_id=1, source_target_pairs={{0,4},{4,8},{8,12},{12,0},{1,5},{5,9},{9,13},{13,1},{2,6},{6,10},{... | collective-permute-start | bytes 3080 | tf_op jit(solution)/shard_map/ppermute | solution.py:26
  64.0 4.8 %collective-permute-start.5 = (f32[256,1]{1,0:T(8,128)S(1)}, f32[256,1]{1,0:T(8,128)S(1)}, u32[]{:S(2)}, u32[]{:S(2)}) collective-permute-start(f32[256,1]{1,0:T(8,128)S(1)} %get-tuple-element.57), channel_id=1, source_target_pairs={{4,0},{8,4},{12,8},{0,12},{5,1},{9,5},{13,9},{1,13},{6,2},{10,6},{... | collective-permute-start | bytes 3080 | tf_op jit(solution)/shard_map/ppermute | solution.py:27
  68.9 5.4 %collective-permute-start.6 = (f32[1,130]{1,0:T(1,128)S(1)}, f32[1,130]{1,0:T(1,128)S(1)}, u32[]{:S(2)}, u32[]{:S(2)}) collective-permute-start(f32[1,130]{1,0:T(1,128)S(1)} %get-tuple-element.47), channel_id=1, source_target_pairs={{0,1},{1,2},{2,3},{3,0},{4,5},{5,6},{6,7},{7,4},{8,9},{9,10},{10,1... | collective-permute-start | bytes 1568 | tf_op jit(solution)/shard_map/ppermute | solution.py:26
  69.5 4.7 %collective-permute-start.7 = (f32[1,130]{1,0:T(1,128)S(1)}, f32[1,130]{1,0:T(1,128)S(1)}, u32[]{:S(2)}, u32[]{:S(2)}) collective-permute-start(f32[1,130]{1,0:T(1,128)S(1)} %get-tuple-element.48), channel_id=1, source_target_pairs={{1,0},{2,1},{3,2},{0,3},{5,4},{6,5},{7,6},{4,7},{9,8},{10,9},{11,1... | collective-permute-start | bytes 1568 | tf_op jit(solution)/shard_map/ppermute | solution.py:27
  111.7 33.5 %copy-start.11 = (f32[256,128]{1,0:T(8,128)}, f32[256,128]{1,0:T(8,128)S(1)}, u32[]{:S(2)}) copy-start(f32[256,128]{1,0:T(8,128)S(1)} %multiply_subtract_fusion.2) | copy-start | bytes 393220
  146.2 4.5 %collective-permute-start.8 = (f32[256,1]{1,0:T(8,128)S(1)}, f32[256,1]{1,0:T(8,128)S(1)}, u32[]{:S(2)}, u32[]{:S(2)}) collective-permute-start(f32[256,1]{1,0:T(8,128)S(1)} %get-tuple-element.54), channel_id=1, source_target_pairs={{0,4},{4,8},{8,12},{12,0},{1,5},{5,9},{9,13},{13,1},{2,6},{6,10},{... | collective-permute-start | bytes 3080 | tf_op jit(solution)/shard_map/ppermute | solution.py:26
  146.3 4.4 %collective-permute-start.9 = (f32[256,1]{1,0:T(8,128)S(1)}, f32[256,1]{1,0:T(8,128)S(1)}, u32[]{:S(2)}, u32[]{:S(2)}) collective-permute-start(f32[256,1]{1,0:T(8,128)S(1)} %get-tuple-element.55), channel_id=1, source_target_pairs={{4,0},{8,4},{12,8},{0,12},{5,1},{9,5},{13,9},{1,13},{6,2},{10,6},{... | collective-permute-start | bytes 3080 | tf_op jit(solution)/shard_map/ppermute | solution.py:27
  150.7 5.4 %collective-permute-start.10 = (f32[1,130]{1,0:T(1,128)S(1)}, f32[1,130]{1,0:T(1,128)S(1)}, u32[]{:S(2)}, u32[]{:S(2)}) collective-permute-start(f32[1,130]{1,0:T(1,128)S(1)} %get-tuple-element.45), channel_id=1, source_target_pairs={{0,1},{1,2},{2,3},{3,0},{4,5},{5,6},{6,7},{7,4},{8,9},{9,10},{10,1... | collective-permute-start | bytes 1568 | tf_op jit(solution)/shard_map/ppermute | solution.py:26
  153.0 3.6 collective-permute-start.11
  228.6 4.5 %collective-permute-start.12 = (f32[256,1]{1,0:T(8,128)S(1)}, f32[256,1]{1,0:T(8,128)S(1)}, u32[]{:S(2)}, u32[]{:S(2)}) collective-permute-start(f32[256,1]{1,0:T(8,128)S(1)} %get-tuple-element.52), channel_id=1, source_target_pairs={{0,4},{4,8},{8,12},{12,0},{1,5},{5,9},{9,13},{13,1},{2,6},{6,10},{... | collective-permute-start | bytes 3080 | tf_op jit(solution)/shard_map/ppermute | solution.py:26
  228.6 4.5 %collective-permute-start.13 = (f32[256,1]{1,0:T(8,128)S(1)}, f32[256,1]{1,0:T(8,128)S(1)}, u32[]{:S(2)}, u32[]{:S(2)}) collective-permute-start(f32[256,1]{1,0:T(8,128)S(1)} %get-tuple-element.53), channel_id=1, source_target_pairs={{4,0},{8,4},{12,8},{0,12},{5,1},{9,5},{13,9},{1,13},{6,2},{10,6},{... | collective-permute-start | bytes 3080 | tf_op jit(solution)/shard_map/ppermute | solution.py:27
  233.2 21.0 %collective-permute-start.14 = (f32[1,130]{1,0:T(1,128)S(1)}, f32[1,130]{1,0:T(1,128)S(1)}, u32[]{:S(2)}, u32[]{:S(2)}) collective-permute-start(f32[1,130]{1,0:T(1,128)S(1)} %get-tuple-element.43), channel_id=1, source_target_pairs={{0,1},{1,2},{2,3},{3,0},{4,5},{5,6},{6,7},{7,4},{8,9},{9,10},{10,1... | collective-permute-start | bytes 1568 | tf_op jit(solution)/shard_map/ppermute | solution.py:26
  235.4 18.8 %collective-permute-start.15 = (f32[1,130]{1,0:T(1,128)S(1)}, f32[1,130]{1,0:T(1,128)S(1)}, u32[]{:S(2)}, u32[]{:S(2)}) collective-permute-start(f32[1,130]{1,0:T(1,128)S(1)} %get-tuple-element.44), channel_id=1, source_target_pairs={{1,0},{2,1},{3,2},{0,3},{5,4},{6,5},{7,6},{4,7},{9,8},{10,9},{11,1... | collective-permute-start | bytes 1568 | tf_op jit(solution)/shard_map/ppermute | solution.py:27
  237.0 17.4 %copy-start.9 = (f32[256,128]{1,0:T(8,128)S(1)}, f32[256,128]{1,0:T(8,128)}, u32[]{:S(2)}) copy-start(f32[256,128]{1,0:T(8,128)} %copy-done.8) | copy-start | bytes 393220
  326.1 11.1 %collective-permute-start.16 = (f32[256,1]{1,0:T(8,128)S(1)}, f32[256,1]{1,0:T(8,128)S(1)}, u32[]{:S(2)}, u32[]{:S(2)}) collective-permute-start(f32[256,1]{1,0:T(8,128)S(1)} %get-tuple-element.50), channel_id=1, source_target_pairs={{0,4},{4,8},{8,12},{12,0},{1,5},{5,9},{9,13},{13,1},{2,6},{6,10},{... | collective-permute-start | bytes 3080 | tf_op jit(solution)/shard_map/ppermute | solution.py:26
  326.2 11.1 %collective-permute-start.17 = (f32[256,1]{1,0:T(8,128)S(1)}, f32[256,1]{1,0:T(8,128)S(1)}, u32[]{:S(2)}, u32[]{:S(2)}) collective-permute-start(f32[256,1]{1,0:T(8,128)S(1)} %get-tuple-element.51), channel_id=1, source_target_pairs={{4,0},{8,4},{12,8},{0,12},{5,1},{9,5},{13,9},{1,13},{6,2},{10,6},{... | collective-permute-start | bytes 3080 | tf_op jit(solution)/shard_map/ppermute | solution.py:27
  337.3 11.7 %collective-permute-start.18 = (f32[1,130]{1,0:T(1,128)S(1)}, f32[1,130]{1,0:T(1,128)S(1)}, u32[]{:S(2)}, u32[]{:S(2)}) collective-permute-start(f32[1,130]{1,0:T(1,128)S(1)} %get-tuple-element.41), channel_id=1, source_target_pairs={{0,1},{1,2},{2,3},{3,0},{4,5},{5,6},{6,7},{7,4},{8,9},{9,10},{10,1... | collective-permute-start | bytes 1568 | tf_op jit(solution)/shard_map/ppermute | solution.py:26
  338.3 10.8 %collective-permute-start.19 = (f32[1,130]{1,0:T(1,128)S(1)}, f32[1,130]{1,0:T(1,128)S(1)}, u32[]{:S(2)}, u32[]{:S(2)}) collective-permute-start(f32[1,130]{1,0:T(1,128)S(1)} %get-tuple-element.42), channel_id=1, source_target_pairs={{1,0},{2,1},{3,2},{0,3},{5,4},{6,5},{7,6},{4,7},{9,8},{10,9},{11,1... | collective-permute-start | bytes 1568 | tf_op jit(solution)/shard_map/ppermute | solution.py:27
  346.1 3.2 copy-start.10
where the time goes:
time: 386 us; the launch traced here: 385 us
  blocking collectives  221 us (57%)
  other arithmetic  74.4 us (19%)
  starting transfers between devices  28.8 us (7%)
  local copies, waits for them, and re-layouts  24.9 us (6%)
  waiting for transfers between devices  18.4 us (5%)
  between operations  10.3 us (3%)
  matrix products  7.75 us (2%)
    psum x4, blocking collectives, residual_product(): return lax.psum(jnp.sum(residual * conditioned), ('lon', 'lat'))  126 us
    psum x3, blocking collectives, local(): lax.psum(jnp.sum(direction * applied), ('lon', 'lat'))  95.1 us
    ppermute x10, starting transfers between devices, padded_2(): after = lax.ppermute(leading, axis, down)  20.8 us
    ppermute x10, waiting for transfers between devices, padded_2(): before = lax.ppermute(last, axis, up)  17.5 us
    add x1, other arithmetic, vertical_shear_part(): face_east * (zonal_mid + zonal_east) * (scalar_middle + scalar_right)  17.2 us
    reduce_sum x1, other arithmetic, local(): transport_cycle_x = jnp.sum(tier_floor[:, None, None] * zonal_cycle, axis=0)  14.4 us
    add x1, other arithmetic, vertical_shear_part(): face_east * (scalar_right - scalar_middle)  9.3 us
    ppermute x10, starting transfers between devices, padded_2(): before = lax.ppermute(last, axis, up)  8.02 us
  transfers between devices with their start and end apart: 20, of which 9 were waited for; matrix products, arithmetic and copies ran while one was open for 10% of the time, Pallas kernels for 0%

commit v1 on v0

v1 whole, which is shorter than its diff:
```python
import functools

import jax
import jax.numpy as jnp
import ml_dtypes
import numpy as np
from jax import lax
from jax.experimental import pallas as pl
from jax.experimental.pallas import tpu as pltpu
from jax.sharding import PartitionSpec as P

BY = 8
ITERS = 4
TIME_STEP = 0.05
DIFFUSIVITY = 0.2
VISCOSITY = 0.2
HEAT_DILATION = 0.5
SURFACE_TERM = 0.01
ROW_DECAY = 0.6
COLUMN_DECAY = 0.6
PAD = 8


def column_operator(extent):
    position = np.arange(extent)
    distance = np.abs(position[:, None] - position[None, :]).astype(np.float64)
    exact = (COLUMN_DECAY**distance).astype(np.float32)
    high = exact.astype(ml_dtypes.bfloat16)
    low = (exact - high.astype(np.float32)).astype(ml_dtypes.bfloat16)
    return np.block([[high, low], [high, np.zeros_like(low)]])


def kernel(
    nx, ny, tiers, rows, cols,
    t_hbm, u_hbm, v_hbm, lev_hbm, op_ref,
    t_out, u_out, v_out, height_ref,
    tpad, upad, vpad, levint, levpad, tnext, unext, vnext,
    txs, typad, sw, dw, le, lw, ln, ls,
    rr, uu, ww, mm, nn, zz, qq, ss, pp,
    ins_s, ins_r, iew_s, iew_r, iew_c,
    sew_s, sew_r, sns_s, sns_r, ar_s, ar_r,
    in_sem, out_sem, ih_send, ih_recv, sh_send, sh_recv, ar_send, ar_recv,
):
    blocks = rows // BY
    pairs = tiers // 2
    fields = (tpad, upad, vpad)
    lon = lax.axis_index("lon")
    lat = lax.axis_index("lat")
    east = {"lon": lax.rem(lon + 1, nx), "lat": lat}
    west = {"lon": lax.rem(lon + nx - 1, nx), "lat": lat}
    north = {"lon": lon, "lat": lat + 1}
    south = {"lon": lon, "lat": lat - 1}
    has_north = lat < ny - 1
    has_south = lat > 0
    peers = [
        {"lon": lax.rem(lon + dx, nx), "lat": lax.rem(lat + dy, ny)}
        for dy in range(ny)
        for dx in range(nx)
        if dx or dy
    ]
    lane = lax.broadcasted_iota(jnp.int32, (BY, cols), 1)
    sub = lax.broadcasted_iota(jnp.int32, (BY, cols), 0)
    odd = lax.rem(lane, 2) == 1
    first = lane == 0
    last = lane == cols - 1
    thick = [2.0 * (k + 1) / (tiers * (tiers + 1)) for k in range(tiers)]

    loads = [
        pltpu.make_async_copy(src, dst, in_sem.at[i])
        for i, (src, dst) in enumerate(
            [
                (lev_hbm, levint),
                (t_hbm, tpad.at[:, pl.ds(PAD, rows), :]),
                (u_hbm, upad.at[:, pl.ds(PAD, rows), :]),
                (v_hbm, vpad.at[:, pl.ds(PAD, rows), :]),
            ]
        )
    ]
    for load in loads:
        load.start()
    ins_r[...] = jnp.zeros_like(ins_r)
    sns_r[...] = jnp.zeros_like(sns_r)
    barrier = pltpu.get_barrier_semaphore()
    for peer in peers:
        pl.semaphore_signal(barrier, inc=1, device_id=peer, device_id_type=pl.DeviceIdType.MESH)
    for load in loads:
        load.wait()
    levpad[pl.ds(PAD, rows), :] = levint[...].astype(jnp.float32)

    def pack_body(j, carry):
        at = pl.multiple_of(PAD + BY * j, BY)
        here = lax.div(lane, 2) == j
        there = lax.div(lane, 2) == j + cols // 4
        out = []
        for f in range(3):
            for h in range(pairs):
                acc = carry[f * pairs + h]
                a = pltpu.roll(fields[f][2 * h, pl.ds(at, BY), :], 2 * j + 1, 1)
                b = pltpu.roll(fields[f][2 * h + 1, pl.ds(at, BY), :], 2 * j + 1 + cols // 2, 1)
                out.append(jnp.where(here, a, jnp.where(there, b, acc)))
        a = pltpu.roll(levpad[pl.ds(at, BY), :], 2 * j + 1, 1)
        out.append(jnp.where(here, a, carry[3 * pairs]))
        return tuple(out)

    zero = jnp.zeros((BY, cols), jnp.float32)
    packed = lax.fori_loop(0, blocks, pack_body, (zero,) * (3 * pairs + 1))
    for i, value in enumerate(packed):
        iew_s[i] = value
    for side, row in ((0, PAD + rows - 1), (1, PAD)):
        for f in range(3):
            for k in range(tiers):
                ins_s[side, pl.ds(f * tiers + k, 1), :] = fields[f][k, pl.ds(row, 1), :]
        ins_s[side, pl.ds(3 * tiers, BY), :] = jnp.broadcast_to(levpad[pl.ds(row, 1), :], (BY, cols))

    def remote(src, dst, send, recv, device):
        return pltpu.make_async_remote_copy(
            src_ref=src, dst_ref=dst, send_sem=send, recv_sem=recv,
            device_id=device, device_id_type=pl.DeviceIdType.MESH,
        )

    pl.semaphore_wait(barrier, len(peers))

    def exchange(ew_src, ew_dst, ns_src, ns_dst, send, recv):
        to_east = remote(ew_src, ew_dst.at[0], send.at[0], recv.at[0], east)
        to_west = remote(ew_src, ew_dst.at[1], send.at[1], recv.at[1], west)
        to_north = remote(ns_src.at[0], ns_dst.at[0], send.at[2], recv.at[2], north)
        to_south = remote(ns_src.at[1], ns_dst.at[1], send.at[3], recv.at[3], south)

        def start():
            to_east.start()
            to_west.start()
            pl.when(has_north)(to_north.start)
            pl.when(has_south)(to_south.start)

        def wait_recv():
            to_east.wait_recv()
            to_west.wait_recv()
            pl.when(has_south)(to_north.wait_recv)
            pl.when(has_north)(to_south.wait_recv)

        def wait_send():
            to_east.wait_send()
            to_west.wait_send()
            pl.when(has_north)(to_north.wait_send)
            pl.when(has_south)(to_south.wait_send)

        return start, wait_recv, wait_send

    finish = []
    start, wait_recv, wait_send = exchange(iew_s, iew_r, ins_s, ins_r, ih_send, ih_recv)
    start()
    finish.append(wait_send)
    wait_recv()
    for side, row in ((0, PAD - 1), (1, PAD + rows)):
        for f in range(3):
            for k in range(tiers):
                fields[f][k, pl.ds(row, 1), :] = ins_r[side, pl.ds(f * tiers + k, 1), :]
        levpad[pl.ds(row, 1), :] = ins_r[side, pl.ds(3 * tiers, 1), :]

    def combine(from_west, from_east):
        return jnp.where(odd, pltpu.roll(from_west, 1, 1), pltpu.roll(from_east, cols - 1, 1))

    for i in range(3 * pairs + 1):
        iew_c[i] = combine(iew_r[0, i], iew_r[1, i])

    def beside(value, halo):
        e = jnp.where(last, halo, pltpu.roll(value, cols - 1, 1))
        w = jnp.where(first, halo, pltpu.roll(value, 1, 1))
        return e, w

    def field_beside(f, k, j, value):
        shift = cols // 2 - 1 - 2 * j + (0 if k % 2 else cols // 2)
        return beside(value, pltpu.roll(iew_c[f * pairs + k // 2], shift, 1))

    def level_beside(j, value):
        return beside(value, pltpu.roll(iew_c[3 * pairs], cols - 1 - 2 * j, 1))

    def faces(j, at):
        lev = levpad[pl.ds(at, BY), :]
        lev_n = levpad[pl.ds(at + 1, BY), :]
        lev_s = levpad[pl.ds(at - 1, BY), :]
        lev_e, lev_w = level_beside(j, lev)
        return lev, lev_e, lev_w, lev_n, lev_s

    total_rows = rows * ny
    depth_scale = 1.0 / (tiers * (tiers + 1))

    def depth(lev):
        return lev * (lev + 1.0) * depth_scale

    def speed_body(j, _):
        at = pl.multiple_of(PAD + BY * j, BY)
        own = pl.multiple_of(BY * j, BY)
        lev, lev_e, lev_w, lev_n, lev_s = faces(j, at)
        me, mw, mn, ms = [jnp.minimum(lev, o) for o in (lev_e, lev_w, lev_n, lev_s)]
        at_row = (lat * rows + own + sub).astype(jnp.float32)
        f = 2.0 * (at_row + 0.5) / total_rows - 1.0
        de = dw_ = dn = ds = zero
        tx = ty = zero
        for k in range(tiers):
            t = tpad[k, pl.ds(at, BY), :]
            u = upad[k, pl.ds(at, BY), :]
            v = vpad[k, pl.ds(at, BY), :]
            te, tw = field_beside(0, k, j, t)
            ue, uw = field_beside(1, k, j, u)
            ve, vw = field_beside(2, k, j, v)
            tn, ts = tpad[k, pl.ds(at + 1, BY), :], tpad[k, pl.ds(at - 1, BY), :]
            un, us = upad[k, pl.ds(at + 1, BY), :], upad[k, pl.ds(at - 1, BY), :]
            vn, vs = vpad[k, pl.ds(at + 1, BY), :], vpad[k, pl.ds(at - 1, BY), :]
            c = -HEAT_DILATION * thick[k]
            de = de + c * (te - t)
            dw_ = dw_ + c * (t - tw)
            dn = dn + c * (tn - t)
            ds = ds + c * (t - ts)
            ke, kw, kn, ks = me > k, mw > k, mn > k, ms > k
            au = (
                jnp.where(ke, VISCOSITY * (ue - u) - 0.5 * de, 0.0)
                + jnp.where(kw, VISCOSITY * (uw - u) - 0.5 * dw_, 0.0)
                + jnp.where(kn, VISCOSITY * (un - u), 0.0)
                + jnp.where(ks, VISCOSITY * (us - u), 0.0)
            )
            av = (
                jnp.where(ke, VISCOSITY * (ve - v), 0.0)
                + jnp.where(kw, VISCOSITY * (vw - v), 0.0)
                + jnp.where(kn, VISCOSITY * (vn - v) - 0.5 * dn, 0.0)
                + jnp.where(ks, VISCOSITY * (vs - v) - 0.5 * ds, 0.0)
            )
            wet = lev > k
            un_ = jnp.where(wet, u + TIME_STEP * (f * v + au), 0.0)
            vn_ = jnp.where(wet, v + TIME_STEP * (av - f * u), 0.0)
            unext[k, pl.ds(own, BY), :] = un_
            vnext[k, pl.ds(own, BY), :] = vn_
            tx = tx + thick[k] * un_
            ty = ty + thick[k] * vn_
        txs[pl.ds(own, BY), :] = tx
        typad[pl.ds(at, BY), :] = ty
        h = depth(lev)
        link = [
            jnp.where(m > 0, 0.5 * (h + depth(o)), 0.0)
            for m, o in ((me, lev_e), (mw, lev_w), (mn, lev_n), (ms, lev_s))
        ]
        diagonal = SURFACE_TERM + link[0] + link[1] + link[2] + link[3]
        surface = lev > 0
        sw[pl.ds(own, BY), :] = jnp.where(surface, 1.0 / jnp.sqrt(diagonal), 0.0)
        dw[pl.ds(own, BY), :] = jnp.where(surface, diagonal, 0.0)
        for ref, value in zip((le, lw, ln, ls), link):
            ref[pl.ds(own, BY), :] = value
        return 0

    lax.fori_loop(0, blocks, speed_body, 0)
    stores = [
        pltpu.make_async_copy(unext, u_out, out_sem.at[0]),
        pltpu.make_async_copy(vnext, v_out, out_sem.at[1]),
        pltpu.make_async_copy(tnext, t_out, out_sem.at[2]),
    ]
    stores[0].start()
    stores[1].start()

    def tracer_body(j, _):
        at = pl.multiple_of(PAD + BY * j, BY)
        own = pl.multiple_of(BY * j, BY)
        lev, lev_e, lev_w, lev_n, lev_s = faces(j, at)
        me, mw, mn, ms = [jnp.minimum(lev, o) for o in (lev_e, lev_w, lev_n, lev_s)]
        for k in range(tiers):
            t = tpad[k, pl.ds(at, BY), :]
            u = upad[k, pl.ds(at, BY), :]
            v = vpad[k, pl.ds(at, BY), :]
            te, tw = field_beside(0, k, j, t)
            ue, uw = field_beside(1, k, j, u)
            tn, ts = tpad[k, pl.ds(at + 1, BY), :], tpad[k, pl.ds(at - 1, BY), :]
            vn, vs = vpad[k, pl.ds(at + 1, BY), :], vpad[k, pl.ds(at - 1, BY), :]
            flow = (
                jnp.where(me > k, DIFFUSIVITY * (te - t) - 0.25 * (u + ue) * (t + te), 0.0)
                + jnp.where(mw > k, DIFFUSIVITY * (tw - t) + 0.25 * (u + uw) * (t + tw), 0.0)
                + jnp.where(mn > k, DIFFUSIVITY * (tn - t) - 0.25 * (v + vn) * (t + tn), 0.0)
                + jnp.where(ms > k, DIFFUSIVITY * (ts - t) + 0.25 * (v + vs) * (t + ts), 0.0)
            )
            tnext[k, pl.ds(own, BY), :] = jnp.where(lev > k, t + TIME_STEP * flow, 0.0)
        return 0

    def tracer_part(part, parts):
        lax.fori_loop(part * blocks // parts, (part + 1) * blocks // parts, tracer_body, 0)

    def block(j):
        return pl.ds(BY * j, BY)

    def send_surface(phase, ew_ref, ns_ref):
        acc = zero
        for j in range(blocks):
            acc = jnp.where(lax.div(lane, 2) == j, pltpu.roll(ew_ref(j), 2 * j + 1, 1), acc)
        sew_s[phase] = acc
        sns_s[phase, 0] = ns_ref[pl.ds(PAD + rows - 1, 1), :]
        sns_s[phase, 1] = ns_ref[pl.ds(PAD, 1), :]
        start, wait_recv, wait_send = exchange(
            sew_s.at[phase], sew_r.at[phase], sns_s.at[phase], sns_r.at[phase],
            sh_send.at[phase], sh_recv.at[phase],
        )
        start()
        finish.append(wait_send)
        return wait_recv

    def halo_of(phase, ns_ref):
        ns_ref[pl.ds(PAD - 1, 1), :] = sns_r[phase, 0]
        ns_ref[pl.ds(PAD + rows, 1), :] = sns_r[phase, 1]
        comb = combine(sew_r[phase, 0], sew_r[phase, 1])
        return lambda j: pltpu.roll(comb, cols - 1 - 2 * j, 1)

    def pad_block(j, move=0):
        return pl.ds(PAD + BY * j + move, BY)

    def operate(phase, ref, out):
        halo = halo_of(phase, ref)
        for j in range(blocks):
            x = ref[pad_block(j), :]
            e, w = beside(x, halo(j))
            out[block(j), :] = dw[block(j), :] * x - (
                le[block(j), :] * e
                + lw[block(j), :] * w
                + ln[block(j), :] * ref[pad_block(j, 1), :]
                + ls[block(j), :] * ref[pad_block(j, -1), :]
            )

    down = [jnp.where(sub >= d, ROW_DECAY**d, 0.0) for d in (1, 2, 4)]
    up = [jnp.where(sub < BY - d, ROW_DECAY**d, 0.0) for d in (1, 2, 4)]

    def condition(src, dst):
        scaled = sw[...] * src[...]
        high = scaled.astype(jnp.bfloat16)
        low = (scaled - high.astype(jnp.float32)).astype(jnp.bfloat16)
        both = jnp.dot(
            jnp.concatenate([high, low], axis=1), op_ref[...], preferred_element_type=jnp.float32
        )
        across = both[:, :cols] + both[:, cols:]
        for j in range(blocks):
            x = across[BY * j : BY * (j + 1), :]
            f = b = x
            for i, d in enumerate((1, 2, 4)):
                f = f + down[i] * pltpu.roll(f, d, 0)
                b = b + up[i] * pltpu.roll(b, BY - d, 0)
            dst[pad_block(j), :] = sw[block(j), :] * (f + b - x)

    wait = send_surface(0, lambda j: txs[block(j), :], typad)
    tracer_part(0, 5)
    wait()
    halo = halo_of(0, typad)
    for j in range(blocks):
        e, w = beside(txs[block(j), :], halo(j))
        r = -0.5 * ((e - w) + (typad[pad_block(j, 1), :] - typad[pad_block(j, -1), :]))
        rr[block(j), :] = jnp.where(levpad[pad_block(j), :] > 0, r, 0.0)
    condition(rr, uu)
    wait = send_surface(1, lambda j: uu[pad_block(j), :], uu)
    tracer_part(1, 5)
    wait()
    operate(1, uu, ww)

    gamma_old = alpha_old = None
    g = d = zero
    for j in range(blocks):
        g = g + rr[block(j), :] * uu[pad_block(j), :]
        d = d + ww[block(j), :] * uu[pad_block(j), :]
    for it in range(ITERS):
        final = it + 1 == ITERS
        both = jnp.where(odd, d + pltpu.roll(d, cols - 1, 1), g + pltpu.roll(g, cols - 1, 1))
        ar_s[it] = jnp.sum(both, axis=0, keepdims=True)
        copies = [
            remote(ar_s.at[it], ar_r.at[it, i], ar_send.at[it], ar_recv.at[it], peer)
            for i, peer in enumerate(peers)
        ]
        for copy in copies:
            copy.start()
        if not final:
            condition(ww, mm)
            wait = send_surface(2 + it, lambda j: mm[pad_block(j), :], mm)
            tracer_part(2 + it, 5)
            if it + 2 == ITERS:
                stores[2].start()
            wait()
            operate(2 + it, mm, nn)
        pltpu.make_async_copy(ar_r.at[it], ar_r.at[it], ar_recv.at[it]).wait()
        total = ar_s[it]
        for i in range(len(peers)):
            total = total + ar_r[it, i]
        total = jnp.broadcast_to(total, (BY, cols))
        step = 2
        while step < cols:
            total = total + pltpu.roll(total, step, 1)
            step *= 2
        gamma = jnp.where(odd, pltpu.roll(total, 1, 1), total)
        delta = jnp.where(odd, total, pltpu.roll(total, cols - 1, 1))
        if it == 0:
            beta = None
            alpha = gamma / delta
        else:
            beta = gamma / gamma_old
            alpha = gamma / (delta - beta * gamma / alpha_old)
        gamma_old, alpha_old = gamma, alpha
        g = d = zero
        for j in range(blocks):
            u = uu[pad_block(j), :]
            p = u if beta is None else u + beta * pp[block(j), :]
            x = alpha * p if it == 0 else height_ref[block(j), :] + alpha * p
            height_ref[block(j), :] = x
            if final:
                continue
            w = ww[block(j), :]
            z, q, s = nn[block(j), :], mm[pad_block(j), :], w
            if beta is not None:
                z = z + beta * zz[block(j), :]
                q = q + beta * qq[block(j), :]
                s = s + beta * ss[block(j), :]
            if it + 2 < ITERS:
                zz[block(j), :] = z
                qq[block(j), :] = q
                ss[block(j), :] = s
            pp[block(j), :] = p
            r = rr[block(j), :] - alpha * s
            u = u - alpha * q
            w = w - alpha * z
            rr[block(j), :] = r
            uu[pad_block(j), :] = u
            ww[block(j), :] = w
            g = g + r * u
            d = d + w * u

    for wait_send in finish:
        wait_send()
    for it in range(ITERS):
        pltpu.make_async_copy(ar_r.at[it], ar_r.at[it], ar_send.at[it]).wait()
    for store in stores:
        store.wait()


def local(heat_anomaly, zonal_speed, meridional_speed, submerged_tiers_per_site):
    tiers, rows, cols = heat_anomaly.shape
    nx, ny = lax.axis_size("lon"), lax.axis_size("lat")
    operator = jnp.asarray(column_operator(cols))
    f32 = jnp.float32
    field = jax.ShapeDtypeStruct((tiers, rows, cols), f32)
    flat = pltpu.VMEM((rows, cols), f32)
    wide = pltpu.VMEM((rows + 2 * PAD, cols), f32)
    wide3 = pltpu.VMEM((tiers, rows + 2 * PAD, cols), f32)
    full3 = pltpu.VMEM((tiers, rows, cols), f32)
    packs = 3 * (tiers // 2) + 1
    lines = 3 * tiers + BY
    phases = ITERS + 1
    others = nx * ny - 1
    any_spec = pl.BlockSpec(memory_space=pl.ANY)
    vmem_spec = pl.BlockSpec(memory_space=pltpu.VMEM)
    dma = pltpu.SemaphoreType.DMA
    return pl.pallas_call(
        functools.partial(kernel, nx, ny, tiers, rows, cols),
        out_shape=(field, field, field, jax.ShapeDtypeStruct((rows, cols), f32)),
        in_specs=[any_spec] * 4 + [vmem_spec],
        out_specs=(any_spec, any_spec, any_spec, vmem_spec),
        scratch_shapes=[
            wide3, wide3, wide3, pltpu.VMEM((rows, cols), jnp.int32), wide, full3, full3, full3,
            flat, wide, flat, flat, flat, flat, flat, flat,
            flat, wide, flat, wide, flat, flat, flat, flat, flat,
            pltpu.VMEM((2, lines, cols), f32),
            pltpu.VMEM((2, lines, cols), f32),
            pltpu.VMEM((packs, BY, cols), f32),
            pltpu.VMEM((2, packs, BY, cols), f32),
            pltpu.VMEM((packs, BY, cols), f32),
            pltpu.VMEM((phases, BY, cols), f32),
            pltpu.VMEM((phases, 2, BY, cols), f32),
            pltpu.VMEM((phases, 2, 1, cols), f32),
            pltpu.VMEM((phases, 2, 1, cols), f32),
            pltpu.VMEM((ITERS, 1, cols), f32),
            pltpu.VMEM((ITERS, others, 1, cols), f32),
            dma((4,)), dma((3,)), dma((4,)), dma((4,)),
            dma((phases, 4)), dma((phases, 4)), dma((ITERS,)), dma((ITERS,)),
        ],
        compiler_params=pltpu.CompilerParams(
            collective_id=0, has_side_effects=True, vmem_limit_bytes=32 * 1024 * 1024
        ),
        name="ocean_step",
    )(heat_anomaly, zonal_speed, meridional_speed, submerged_tiers_per_site, operator)


def solution(mesh):
    placed = (
        P("groups", "lat", "lon"),
        P("groups", "lat", "lon"),
        P("groups", "lat", "lon"),
        P(("groups", "lat"), "lon"),
    )
    return jax.shard_map(
        local,
        mesh=mesh,
        in_specs=placed,
        out_specs=placed,
        check_vma=False,
    )
```

time: 386 us -> 49.5 us (0.13)
  blocking collectives: 221 us -> 0 us
  other arithmetic: 74.4 us -> 0 us
  Pallas kernels: 0 us -> 39.6 us
  starting transfers between devices: 28.8 us -> 0 us
  waiting for transfers between devices: 18.4 us -> 0 us
  local copies, waits for them, and re-layouts: 24.9 us -> 9.04 us
  between operations: 10.3 us -> 0.65 us
  matrix products: 7.75 us -> 0 us
    psum x7 -> x0, blocking collectives: 221 us -> none  [the longest x4 126 us: residual_product(): return lax.psum(jnp.sum(residual * conditioned), ('lon', 'lat'))]
    pallas_call x0 -> x1, Pallas kernels: none -> 39.6 us  [local(): pl.pallas_call(functools.partial(kernel, nx, ny, tiers, rows, cols), out_...]
    add x6 -> x0, other arithmetic: 29.9 us -> none  [the longest x1 17.2 us: vertical_shear_part(): face_east * (zonal_mid + zonal_east) * (scalar_middle + scalar_right)]
    ppermute x20 -> x0, starting transfers between devices: 28.8 us -> none  [the longest x10 20.8 us: padded_2(): after = lax.ppermute(leading, axis, down)]
    reduce_sum x5 -> x0, other arithmetic: 19.6 us -> none  [the longest x1 14.4 us: local(): transport_cycle_x = jnp.sum(tier_floor[:, None, None] * zonal_cycle, axis=0)]
    ppermute x20 -> x0, waiting for transfers between devices: 18.4 us -> none  [the longest x10 17.5 us: padded_2(): before = lax.ppermute(last, axis, up)]
    slice x9 -> x0, local copies, waits for them, and re-layouts: 16.6 us -> none  [the longest x6 7.92 us: padded_2(): last = lax.slice_in_dim(array, length - width, length, axis=dim)]
    mul x8 -> x0, other arithmetic: 16.2 us -> none  [the longest x1 7.6 us: local(): extended = extended * wide_valid[None, None, :, None]]
  transfers between devices with their start and end apart: 20 -> 0, of which waited for: 9 -> 0; matrix products, arithmetic and copies ran while one was open for 10% -> 0% of each run, Pallas kernels for 0% -> 0%
where the time goes in v1:
time: 49.5 us; the launch traced here: 49.3 us
  Pallas kernels  39.6 us (80%)
  local copies, waits for them, and re-layouts  9.04 us (18%)
  between operations  0.65 us (1%)
    pallas_call x1, Pallas kernels, local(): pl.pallas_call(functools.partial(kernel, nx, ny, tiers, rows, cols), out_...  39.6 us
    unnamed x14, local copies, waits for them, and re-layouts  9.04 us

profile of v1, /device:TPU:0, one launch (start us, length us, event | category | flops | bytes accessed | tf_op | source)
XLA Modules:
  0.0 49.3 jit_solution(15542394408434003235)
XLA Ops:
  0.6 0.0 copy-start
  0.6 1.2 %copy-done = f32[8,256,128]{2,1,0:T(8,128)S(1)} copy-done((f32[8,256,128]{2,1,0:T(8,128)S(1)}, f32[8,256,128]{2,1,0:T(8,128)}, u32[]{:S(2)}) %copy-start) | copy-done | bytes 1048600
  1.9 0.0 copy-start.1
  1.9 1.2 %copy-done.1 = f32[8,256,128]{2,1,0:T(8,128)S(1)} copy-done((f32[8,256,128]{2,1,0:T(8,128)S(1)}, f32[8,256,128]{2,1,0:T(8,128)}, u32[]{:S(2)}) %copy-start.1) | copy-done | bytes 1048600
  3.1 0.0 copy-start.2
  3.1 1.2 %copy-done.2 = f32[8,256,128]{2,1,0:T(8,128)S(1)} copy-done((f32[8,256,128]{2,1,0:T(8,128)S(1)}, f32[8,256,128]{2,1,0:T(8,128)}, u32[]{:S(2)}) %copy-start.2) | copy-done | bytes 1048600
  4.3 0.0 copy-start.3
  4.3 0.9 %copy-done.3 = s32[256,128]{1,0:T(8,128)S(1)} copy-done((s32[256,128]{1,0:T(8,128)S(1)}, s32[256,128]{1,0:T(8,128)}, u32[]{:S(2)}) %copy-start.3) | copy-done | bytes 131096
  5.2 0.0 copy-start.4
  5.2 0.9 %copy-done.4 = bf16[256,256]{1,0:T(8,128)(2,1)S(1)} copy-done((bf16[256,256]{1,0:T(8,128)(2,1)S(1)}, bf16[256,256]{1,0:T(8,128)(2,1)}, u32[]{:S(2)}) %copy-start.4) | copy-done | bytes 131096
  6.1 39.6 %ocean_step.1 = (f32[8,256,128]{2,1,0:T(8,128)S(1)}, f32[8,256,128]{2,1,0:T(8,128)S(1)}, f32[8,256,128]{2,1,0:T(8,128)S(1)}, f32[256,128]{1,0:T(8,128)S(1)}) custom-call(f32[8,256,128]{2,1,0:T(8,128)S(1)} %copy-done, f32[8,256,128]{2,1,0:T(8,128)S(1)} %copy-done.1, f32[8,256,128]{2,1,0:T(8,128)S(1)} %copy-done.2, s32[256,128]{1,0:T(8,128)S(1)} %copy-done.3, ...), custom_call_target="tpu_custom_call" | custom-call | tf_op jit(solution)/shard_map/ocean_step/pallas_call | solution.py:450
  45.7 1.0 %copy.13 = f32[8,256,128]{2,1,0:T(8,128)} copy(f32[8,256,128]{2,1,0:T(8,128)S(1)} %get-tuple-element.8) | data formatting | bytes 2097152
  46.7 1.0 %copy.14 = f32[8,256,128]{2,1,0:T(8,128)} copy(f32[8,256,128]{2,1,0:T(8,128)S(1)} %get-tuple-element.9) | data formatting | bytes 2097152
  47.6 1.0 %copy.15 = f32[8,256,128]{2,1,0:T(8,128)} copy(f32[8,256,128]{2,1,0:T(8,128)S(1)} %get-tuple-element.10) | data formatting | bytes 2097152
  48.6 0.7 %copy.16 = f32[256,128]{1,0:T(8,128)} copy(f32[256,128]{1,0:T(8,128)S(1)} %get-tuple-element.11) | data formatting | bytes 262144
Async XLA Ops:
  0.6 1.2 %copy-start = (f32[8,256,128]{2,1,0:T(8,128)S(1)}, f32[8,256,128]{2,1,0:T(8,128)}, u32[]{:S(2)}) copy-start(f32[8,256,128]{2,1,0:T(8,128)} %t_hbm.1) | copy-start | bytes 3145732
  1.9 1.2 %copy-start.1 = (f32[8,256,128]{2,1,0:T(8,128)S(1)}, f32[8,256,128]{2,1,0:T(8,128)}, u32[]{:S(2)}) copy-start(f32[8,256,128]{2,1,0:T(8,128)} %u_hbm.1) | copy-start | bytes 3145732
  3.1 1.2 %copy-start.2 = (f32[8,256,128]{2,1,0:T(8,128)S(1)}, f32[8,256,128]{2,1,0:T(8,128)}, u32[]{:S(2)}) copy-start(f32[8,256,128]{2,1,0:T(8,128)} %v_hbm.1) | copy-start | bytes 3145732
  4.3 0.9 %copy-start.3 = (s32[256,128]{1,0:T(8,128)S(1)}, s32[256,128]{1,0:T(8,128)}, u32[]{:S(2)}) copy-start(s32[256,128]{1,0:T(8,128)} %lev_hbm.1) | copy-start | bytes 393220
  5.2 0.9 %copy-start.4 = (bf16[256,256]{1,0:T(8,128)(2,1)S(1)}, bf16[256,256]{1,0:T(8,128)(2,1)}, u32[]{:S(2)}) copy-start(bf16[256,256]{1,0:T(8,128)(2,1)} %constant.2.clone.op_ref) | copy-start | bytes 393220

commit v2 on v1

--- a/solution.py
+++ b/solution.py
@@ -19,6 +19,9 @@
 ROW_DECAY = 0.6
 COLUMN_DECAY = 0.6
 PAD = 8
+CENTRE = 1.2
+RADIUS = 1.2
+SLOTS = 16
 
 
 def column_operator(extent):
@@ -33,16 +36,17 @@
 def kernel(
     nx, ny, tiers, rows, cols,
     t_hbm, u_hbm, v_hbm, lev_hbm, op_ref,
-    t_out, u_out, v_out, height_ref,
-    tpad, upad, vpad, levint, levpad, tnext, unext, vnext,
+    tnext, unext, vnext, height_ref,
+    tpad, upad, vpad, levint, levpad,
     txs, typad, sw, dw, le, lw, ln, ls,
-    rr, uu, ww, mm, nn, zz, qq, ss, pp,
+    rr, b0, b1, b2, b3, a0, a1, a2, a3,
     ins_s, ins_r, iew_s, iew_r, iew_c,
     sew_s, sew_r, sns_s, sns_r, ar_s, ar_r,
-    in_sem, out_sem, ih_send, ih_recv, sh_send, sh_recv, ar_send, ar_recv,
+    in_sem, ih_send, ih_recv, sh_send, sh_recv, ar_send, ar_recv,
 ):
     blocks = rows // BY
     pairs = tiers // 2
+    basis, images = (b0, b1, b2, b3), (a0, a1, a2, a3)
     fields = (tpad, upad, vpad)
     lon = lax.axis_index("lon")
     lat = lax.axis_index("lat")
@@ -248,14 +252,6 @@
         return 0
 
     lax.fori_loop(0, blocks, speed_body, 0)
-    stores = [
-        pltpu.make_async_copy(unext, u_out, out_sem.at[0]),
-        pltpu.make_async_copy(vnext, v_out, out_sem.at[1]),
-        pltpu.make_async_copy(tnext, t_out, out_sem.at[2]),
-    ]
-    stores[0].start()
-    stores[1].start()
-
     def tracer_body(j, _):
         at = pl.multiple_of(PAD + BY * j, BY)
         own = pl.multiple_of(BY * j, BY)
@@ -323,7 +319,7 @@
     down = [jnp.where(sub >= d, ROW_DECAY**d, 0.0) for d in (1, 2, 4)]
     up = [jnp.where(sub < BY - d, ROW_DECAY**d, 0.0) for d in (1, 2, 4)]
 
-    def condition(src, dst):
+    def condition(src, dst, scale=1.0, minus=()):
         scaled = sw[...] * src[...]
         high = scaled.astype(jnp.bfloat16)
         low = (scaled - high.astype(jnp.float32)).astype(jnp.bfloat16)
@@ -337,7 +333,10 @@
             for i, d in enumerate((1, 2, 4)):
                 f = f + down[i] * pltpu.roll(f, d, 0)
                 b = b + up[i] * pltpu.roll(b, BY - d, 0)
-            dst[pad_block(j), :] = sw[block(j), :] * (f + b - x)
+            y = scale * sw[block(j), :] * (f + b - x)
+            for factor, ref in minus:
+                y = y - factor * ref[pad_block(j), :]
+            dst[pad_block(j), :] = y
 
     wait = send_surface(0, lambda j: txs[block(j), :], typad)
     tracer_part(0, 5)
@@ -347,87 +346,133 @@
         e, w = beside(txs[block(j), :], halo(j))
         r = -0.5 * ((e - w) + (typad[pad_block(j, 1), :] - typad[pad_block(j, -1), :]))
         rr[block(j), :] = jnp.where(levpad[pad_block(j), :] > 0, r, 0.0)
-    condition(rr, uu)
-    wait = send_surface(1, lambda j: uu[pad_block(j), :], uu)
-    tracer_part(1, 5)
-    wait()
-    operate(1, uu, ww)
-
-    gamma_old = alpha_old = None
-    g = d = zero
+    def dot(a, b):
+        acc = zero
+        for j in range(blocks):
+            acc = acc + a(j) * b(j)
+        return acc
+
+    def at_block(ref):
+        return lambda j: ref[block(j), :]
+
+    def at_pad(ref):
+        return lambda j: ref[pad_block(j), :]
+
+    sums = {}
+    for k in range(ITERS):
+        if k == 0:
+            condition(rr, basis[0])
+        elif k == 1:
+            condition(images[0], basis[1], 1.0 / RADIUS, ((CENTRE / RADIUS, basis[0]),))
+        else:
+            condition(
+                images[k - 1], basis[k], 2.0 / RADIUS,
+                ((2.0 * CENTRE / RADIUS, basis[k - 1]), (1.0, basis[k - 2])),
+            )
+        wait = send_surface(k + 1, at_pad(basis[k]), basis[k])
+        sums["f", k] = dot(at_block(rr), at_pad(basis[k]))
+        for i in range(k):
+            sums[i, k] = dot(at_block(images[i]), at_pad(basis[k]))
+        if k:
+            sums[k - 1, k - 1] = dot(at_block(images[k - 1]), at_pad(basis[k - 1]))
+        tracer_part(k + 1, ITERS + 1)
+        if k + 1 == ITERS:
+            keys = list(sums)
+            tiles = [sums[key] for key in keys]
+            tiles += [zero] * (SLOTS - len(tiles))
+            width = 1
+            while len(tiles) > 1:
+                upper = lax.rem(lax.div(lane, width), 2) == 1
+                half = len(tiles) // 2
+                tiles = [
+                    jnp.where(
+                        upper,
+                        tiles[i + half] + pltpu.roll(tiles[i + half], width, 1),
+                        tiles[i] + pltpu.roll(tiles[i], cols - width, 1),
+                    )
+                    for i in range(half)
+                ]
+                width *= 2
+            early = tiles[0]
+        wait()
+        operate(k + 1, basis[k], images[k])
+    late = dot(at_block(images[-1]), at_pad(basis[-1]))
+    width = 1
+    while width < SLOTS:
+        late = late + pltpu.roll(late, width, 1)
+        width *= 2
+    keys.append((ITERS - 1, ITERS - 1))
+
+    def slot_of(i):
+        at, bits = 0, SLOTS // 2
+        width = 1
+        while bits:
+            at += width if i & bits else 0
+            width *= 2
+            bits //= 2
+        return at
+
+    final = slot_of(len(keys) - 1)
+    both = jnp.where(lax.rem(lane, SLOTS) == final, late, early)
+    ar_s[...] = jnp.sum(both, axis=0, keepdims=True)
+    copies = [
+        remote(ar_s, ar_r.at[i], ar_send.at[0], ar_recv.at[0], peer) for i, peer in enumerate(peers)
+    ]
+    for copy in copies:
+        copy.start()
+    pltpu.make_async_copy(ar_r, ar_r, ar_recv.at[0]).wait()
+    total = ar_s[...]
+    for i in range(len(peers)):
+        total = total + ar_r[i]
+    total = jnp.broadcast_to(total, (BY, cols))
+    width = SLOTS
+    while width < cols:
+        total = total + pltpu.roll(total, width, 1)
+        width *= 2
+    value = {}
+    for i, key in enumerate(keys):
+        at = slot_of(i)
+        value[key] = jnp.broadcast_to(total[:, at : at + 1], (BY, cols))
+    gram = {(i, j): value[i, j] for j in range(ITERS) for i in range(j + 1)}
+    rhs = [value["f", k] for k in range(ITERS)]
+    floor = [1e-6 * gram[i, i] for i in range(ITERS)]
+    inverse = []
+    for i in range(ITERS):
+        pivot = gram[i, i]
+        usable = pivot > floor[i]
+        inverse.append(jnp.where(usable, 1.0 / jnp.where(usable, pivot, 1.0), 0.0))
+        for j in range(i + 1, ITERS):
+            factor = gram[i, j] * inverse[i]
+            rhs[j] = rhs[j] - factor * rhs[i]
+            for k in range(j, ITERS):
+                gram[j, k] = gram[j, k] - factor * gram[i, k]
+    weights = [None] * ITERS
+    for i in reversed(range(ITERS)):
+        acc = rhs[i]
+        for j in range(i + 1, ITERS):
+            acc = acc - gram[i, j] * weights[j]
+        weights[i] = acc * inverse[i]
     for j in range(blocks):
-        g = g + rr[block(j), :] * uu[pad_block(j), :]
-        d = d + ww[block(j), :] * uu[pad_block(j), :]
-    for it in range(ITERS):
-        final = it + 1 == ITERS
-        both = jnp.where(odd, d + pltpu.roll(d, cols - 1, 1), g + pltpu.roll(g, cols - 1, 1))
-        ar_s[it] = jnp.sum(both, axis=0, keepdims=True)
-        copies = [
-            remote(ar_s.at[it], ar_r.at[it, i], ar_send.at[it], ar_recv.at[it], peer)
-            for i, peer in enumerate(peers)
-        ]
-        for copy in copies:
-            copy.start()
-        if not final:
-            condition(ww, mm)
-            wait = send_surface(2 + it, lambda j: mm[pad_block(j), :], mm)
-            tracer_part(2 + it, 5)
-            if it + 2 == ITERS:
-                stores[2].start()
-            wait()
-            operate(2 + it, mm, nn)
-        pltpu.make_async_copy(ar_r.at[it], ar_r.at[it], ar_recv.at[it]).wait()
-        total = ar_s[it]
-        for i in range(len(peers)):
-            total = total + ar_r[it, i]
-        total = jnp.broadcast_to(total, (BY, cols))
-        step = 2
-        while step < cols:
-            total = total + pltpu.roll(total, step, 1)
-            step *= 2
-        gamma = jnp.where(odd, pltpu.roll(total, 1, 1), total)
-        delta = jnp.where(odd, total, pltpu.roll(total, cols - 1, 1))
-        if it == 0:
-            beta = None
-            alpha = gamma / delta
-        else:
-            beta = gamma / gamma_old
-            alpha = gamma / (delta - beta * gamma / alpha_old)
-        gamma_old, alpha_old = gamma, alpha
-        g = d = zero
-        for j in range(blocks):
-            u = uu[pad_block(j), :]
-            p = u if beta is None else u + beta * pp[block(j), :]
-            x = alpha * p if it == 0 else height_ref[block(j), :] + alpha * p
-            height_ref[block(j), :] = x
-            if final:
-                continue
-            w = ww[block(j), :]
-            z, q, s = nn[block(j), :], mm[pad_block(j), :], w
-            if beta is not None:
-                z = z + beta * zz[block(j), :]
-                q = q + beta * qq[block(j), :]
-                s = s + beta * ss[block(j), :]
-            if it + 2 < ITERS:
-                zz[block(j), :] = z
-                qq[block(j), :] = q
-                ss[block(j), :] = s
-            pp[block(j), :] = p
-            r = rr[block(j), :] - alpha * s
-            u = u - alpha * q
-            w = w - alpha * z
-            rr[block(j), :] = r
-            uu[pad_block(j), :] = u
-            ww[block(j), :] = w
-            g = g + r * u
-            d = d + w * u
+        x = weights[0] * basis[0][pad_block(j), :]
+        for k in range(1, ITERS):
+            x = x + weights[k] * basis[k][pad_block(j), :]
+        height_ref[block(j), :] = x
 
     for wait_send in finish:
         wait_send()
-    for it in range(ITERS):
-        pltpu.make_async_copy(ar_r.at[it], ar_r.at[it], ar_send.at[it]).wait()
-    for store in stores:
-        store.wait()
+    pltpu.make_async_copy(ar_r, ar_r, ar_send.at[0]).wait()
+
+
+def write_kernel(*refs):
+    sources, targets, sem = refs[:4], refs[4:8], refs[8]
+    copies = [
+        pltpu.make_async_copy(source, target, sem.at[i])
+        for i, (source, target) in enumerate(zip(sources, targets))
+    ]
+    for copy in copies:
+        copy.start()
+    for copy in copies:
+        copy.wait()
 
 
 def local(heat_anomaly, zonal_speed, meridional_speed, submerged_tiers_per_site):
@@ -436,10 +481,10 @@
     operator = jnp.asarray(column_operator(cols))
     f32 = jnp.float32
     field = jax.ShapeDtypeStruct((tiers, rows, cols), f32)
+    shapes = (field, field, field, jax.ShapeDtypeStruct((rows, cols), f32))
     flat = pltpu.VMEM((rows, cols), f32)
     wide = pltpu.VMEM((rows + 2 * PAD, cols), f32)
     wide3 = pltpu.VMEM((tiers, rows + 2 * PAD, cols), f32)
-    full3 = pltpu.VMEM((tiers, rows, cols), f32)
     packs = 3 * (tiers // 2) + 1
     lines = 3 * tiers + BY
     phases = ITERS + 1
@@ -447,15 +492,15 @@
     any_spec = pl.BlockSpec(memory_space=pl.ANY)
     vmem_spec = pl.BlockSpec(memory_space=pltpu.VMEM)
     dma = pltpu.SemaphoreType.DMA
-    return pl.pallas_call(
+    results = pl.pallas_call(
         functools.partial(kernel, nx, ny, tiers, rows, cols),
-        out_shape=(field, field, field, jax.ShapeDtypeStruct((rows, cols), f32)),
+        out_shape=shapes,
         in_specs=[any_spec] * 4 + [vmem_spec],
-        out_specs=(any_spec, any_spec, any_spec, vmem_spec),
+        out_specs=(vmem_spec,) * 4,
         scratch_shapes=[
-            wide3, wide3, wide3, pltpu.VMEM((rows, cols), jnp.int32), wide, full3, full3, full3,
+            wide3, wide3, wide3, pltpu.VMEM((rows, cols), jnp.int32), wide,
             flat, wide, flat, flat, flat, flat, flat, flat,
-            flat, wide, flat, wide, flat, flat, flat, flat, flat,
+            flat, wide, wide, wide, wide, flat, flat, flat, flat,
             pltpu.VMEM((2, lines, cols), f32),
             pltpu.VMEM((2, lines, cols), f32),
             pltpu.VMEM((packs, BY, cols), f32),
@@ -465,16 +510,24 @@
             pltpu.VMEM((phases, 2, BY, cols), f32),
             pltpu.VMEM((phases, 2, 1, cols), f32),
             pltpu.VMEM((phases, 2, 1, cols), f32),
-            pltpu.VMEM((ITERS, 1, cols), f32),
-            pltpu.VMEM((ITERS, others, 1, cols), f32),
-            dma((4,)), dma((3,)), dma((4,)), dma((4,)),
-            dma((phases, 4)), dma((phases, 4)), dma((ITERS,)), dma((ITERS,)),
+            pltpu.VMEM((1, cols), f32),
+            pltpu.VMEM((others, 1, cols), f32),
+            dma((4,)), dma((4,)), dma((4,)),
+            dma((phases, 4)), dma((phases, 4)), dma((1,)), dma((1,)),
         ],
         compiler_params=pltpu.CompilerParams(
-            collective_id=0, has_side_effects=True, vmem_limit_bytes=32 * 1024 * 1024
+            collective_id=0, has_side_effects=True, vmem_limit_bytes=60 * 1024 * 1024
         ),
         name="ocean_step",
     )(heat_anomaly, zonal_speed, meridional_speed, submerged_tiers_per_site, operator)
+    return pl.pallas_call(
+        write_kernel,
+        out_shape=shapes,
+        in_specs=[vmem_spec] * 4,
+        out_specs=(any_spec,) * 4,
+        scratch_shapes=[dma((4,))],
+        name="write_results",
+    )(*results)
 
 
 def solution(mesh):

time: 49.5 us -> 43.5 us (0.88)
  local copies, waits for them, and re-layouts: 9.04 us -> 0 us
  Pallas kernels: 39.6 us -> 42.7 us
    unnamed x14 -> x0, local copies, waits for them, and re-layouts: 9.04 us -> none
    pallas_call x0 -> x1, Pallas kernels: none -> 3.59 us  [local(): pl.pallas_call(write_kernel, out_shape=shapes, in_specs=[vmem_spec] * 4,...]
where the time goes in v2:
time: 43.5 us; the launch traced here: 43.3 us
  Pallas kernels  42.7 us (98%)
  between operations  0.64 us (1%)
    pallas_call x1, Pallas kernels, local(): pl.pallas_call(functools.partial(kernel, nx, ny, tiers, rows, cols), out_...  39.1 us
    pallas_call x1, Pallas kernels, local(): pl.pallas_call(write_kernel, out_shape=shapes, in_specs=[vmem_spec] * 4,...  3.59 us

profile of v2, /device:TPU:0, one launch (start us, length us, event | category | flops | bytes accessed | tf_op | source)
XLA Modules:
  0.0 43.3 jit_solution(1023383205591926690)
XLA Ops:
  0.6 39.1 %ocean_step.1 = (f32[8,256,128]{2,1,0:T(8,128)}, f32[8,256,128]{2,1,0:T(8,128)}, f32[8,256,128]{2,1,0:T(8,128)}, f32[256,128]{1,0:T(8,128)}) custom-call(f32[8,256,128]{2,1,0:T(8,128)} %t_hbm.1, f32[8,256,128]{2,1,0:T(8,128)} %u_hbm.1, f32[8,256,128]{2,1,0:T(8,128)} %v_hbm.1, s32[256,128]{1,0:T(8,128)} %lev_hbm.1, bf16[256,256]{1,0:T(8,128)(2,1)} %constant.2.clone.op_ref), custom_call_target="tpu_custom_call" | custom-call | tf_op jit(solution)/shard_map/ocean_step/pallas_call | solution.py:495
  39.8 3.6 %write_results.1 = (f32[8,256,128]{2,1,0:T(8,128)}, f32[8,256,128]{2,1,0:T(8,128)}, f32[8,256,128]{2,1,0:T(8,128)}, f32[256,128]{1,0:T(8,128)}) custom-call(f32[8,256,128]{2,1,0:T(8,128)} %get-tuple-element.8.refs_0_, f32[8,256,128]{2,1,0:T(8,128)} %get-tuple-element.9.refs_1_, f32[8,256,128]{2,1,0:T(8,128)} %get-tuple-element.10.refs_2_, ...), custom_call_target="tpu_custom_call" | custom-call | tf_op jit(solution)/shard_map/write_results/pallas_call | solution.py:523

commit v3 on v2

--- a/solution.py
+++ b/solution.py
@@ -65,6 +65,7 @@
     lane = lax.broadcasted_iota(jnp.int32, (BY, cols), 1)
     sub = lax.broadcasted_iota(jnp.int32, (BY, cols), 0)
     odd = lax.rem(lane, 2) == 1
+    zero = jnp.zeros((BY, cols), jnp.float32)
     first = lane == 0
     last = lane == cols - 1
     thick = [2.0 * (k + 1) / (tiers * (tiers + 1)) for k in range(tiers)]
@@ -83,6 +84,8 @@
     for load in loads:
         load.start()
     ins_r[...] = jnp.zeros_like(ins_r)
+    levpad[pl.ds(0, PAD), :] = zero
+    levpad[pl.ds(PAD + rows, PAD), :] = zero
     sns_r[...] = jnp.zeros_like(sns_r)
     barrier = pltpu.get_barrier_semaphore()
     for peer in peers:
@@ -106,7 +109,6 @@
         out.append(jnp.where(here, a, carry[3 * pairs]))
         return tuple(out)
 
-    zero = jnp.zeros((BY, cols), jnp.float32)
     packed = lax.fori_loop(0, blocks, pack_body, (zero,) * (3 * pairs + 1))
     for i, value in enumerate(packed):
         iew_s[i] = value
@@ -154,80 +156,62 @@
     start, wait_recv, wait_send = exchange(iew_s, iew_r, ins_s, ins_r, ih_send, ih_recv)
     start()
     finish.append(wait_send)
-    wait_recv()
-    for side, row in ((0, PAD - 1), (1, PAD + rows)):
-        for f in range(3):
-            for k in range(tiers):
-                fields[f][k, pl.ds(row, 1), :] = ins_r[side, pl.ds(f * tiers + k, 1), :]
-        levpad[pl.ds(row, 1), :] = ins_r[side, pl.ds(3 * tiers, 1), :]
-
-    def combine(from_west, from_east):
-        return jnp.where(odd, pltpu.roll(from_west, 1, 1), pltpu.roll(from_east, cols - 1, 1))
-
-    for i in range(3 * pairs + 1):
-        iew_c[i] = combine(iew_r[0, i], iew_r[1, i])
-
-    def beside(value, halo):
-        e = jnp.where(last, halo, pltpu.roll(value, cols - 1, 1))
-        w = jnp.where(first, halo, pltpu.roll(value, 1, 1))
-        return e, w
-
-    def field_beside(f, k, j, value):
-        shift = cols // 2 - 1 - 2 * j + (0 if k % 2 else cols // 2)
-        return beside(value, pltpu.roll(iew_c[f * pairs + k // 2], shift, 1))
-
-    def level_beside(j, value):
-        return beside(value, pltpu.roll(iew_c[3 * pairs], cols - 1 - 2 * j, 1))
-
-    def faces(j, at):
-        lev = levpad[pl.ds(at, BY), :]
-        lev_n = levpad[pl.ds(at + 1, BY), :]
-        lev_s = levpad[pl.ds(at - 1, BY), :]
-        lev_e, lev_w = level_beside(j, lev)
-        return lev, lev_e, lev_w, lev_n, lev_s
-
     total_rows = rows * ny
     depth_scale = 1.0 / (tiers * (tiers + 1))
+    edge = first | last
+    high_half = lane >= cols // 2
 
     def depth(lev):
         return lev * (lev + 1.0) * depth_scale
 
-    def speed_body(j, _):
+    def inner_faces(at):
+        lev = levpad[pl.ds(at, BY), :]
+        lev_e = jnp.where(last, 0.0, pltpu.roll(lev, cols - 1, 1))
+        me = jnp.minimum(lev, lev_e)
+        mn = jnp.minimum(lev, levpad[pl.ds(at + 1, BY), :])
+        ms = jnp.minimum(lev, levpad[pl.ds(at - 1, BY), :])
+        return lev, me, mn, ms
+
+    def east_of(value):
+        return pltpu.roll(value, cols - 1, 1)
+
+    def west_of(value):
+        return pltpu.roll(value, 1, 1)
+
+    def speed_body(j, carry):
         at = pl.multiple_of(PAD + BY * j, BY)
         own = pl.multiple_of(BY * j, BY)
-        lev, lev_e, lev_w, lev_n, lev_s = faces(j, at)
-        me, mw, mn, ms = [jnp.minimum(lev, o) for o in (lev_e, lev_w, lev_n, lev_s)]
+        lev, me, mn, ms = inner_faces(at)
         at_row = (lat * rows + own + sub).astype(jnp.float32)
         f = 2.0 * (at_row + 0.5) / total_rows - 1.0
-        de = dw_ = dn = ds = zero
+        de = dn = ds = zero
         tx = ty = zero
         for k in range(tiers):
             t = tpad[k, pl.ds(at, BY), :]
             u = upad[k, pl.ds(at, BY), :]
             v = vpad[k, pl.ds(at, BY), :]
-            te, tw = field_beside(0, k, j, t)
-            ue, uw = field_beside(1, k, j, u)
-            ve, vw = field_beside(2, k, j, v)
             tn, ts = tpad[k, pl.ds(at + 1, BY), :], tpad[k, pl.ds(at - 1, BY), :]
             un, us = upad[k, pl.ds(at + 1, BY), :], upad[k, pl.ds(at - 1, BY), :]
             vn, vs = vpad[k, pl.ds(at + 1, BY), :], vpad[k, pl.ds(at - 1, BY), :]
-            c = -HEAT_DILATION * thick[k]
-            de = de + c * (te - t)
-            dw_ = dw_ + c * (t - tw)
+            c = -0.5 * HEAT_DILATION * thick[k]
+            de = de + c * (east_of(t) - t)
             dn = dn + c * (tn - t)
             ds = ds + c * (t - ts)
-            ke, kw, kn, ks = me > k, mw > k, mn > k, ms > k
+            ke, kn, ks = me > k, mn > k, ms > k
+            gu = jnp.where(ke, VISCOSITY * (east_of(u) - u), 0.0)
+            gv = jnp.where(ke, VISCOSITY * (east_of(v) - v), 0.0)
+            gp = jnp.where(ke, de, 0.0)
             au = (
-                jnp.where(ke, VISCOSITY * (ue - u) - 0.5 * de, 0.0)
-                + jnp.where(kw, VISCOSITY * (uw - u) - 0.5 * dw_, 0.0)
+                (gu - gp)
+                - west_of(gu + gp)
                 + jnp.where(kn, VISCOSITY * (un - u), 0.0)
                 + jnp.where(ks, VISCOSITY * (us - u), 0.0)
             )
             av = (
-                jnp.where(ke, VISCOSITY * (ve - v), 0.0)
-                + jnp.where(kw, VISCOSITY * (vw - v), 0.0)
-                + jnp.where(kn, VISCOSITY * (vn - v) - 0.5 * dn, 0.0)
-                + jnp.where(ks, VISCOSITY * (vs - v) - 0.5 * ds, 0.0)
+                gv
+                - west_of(gv)
+                + jnp.where(kn, VISCOSITY * (vn - v) - dn, 0.0)
+                + jnp.where(ks, VISCOSITY * (vs - v) - ds, 0.0)
             )
             wet = lev > k
             un_ = jnp.where(wet, u + TIME_STEP * (f * v + au), 0.0)
@@ -238,41 +222,109 @@
             ty = ty + thick[k] * vn_
         txs[pl.ds(own, BY), :] = tx
         typad[pl.ds(at, BY), :] = ty
-        h = depth(lev)
-        link = [
-            jnp.where(m > 0, 0.5 * (h + depth(o)), 0.0)
-            for m, o in ((me, lev_e), (mw, lev_w), (mn, lev_n), (ms, lev_s))
-        ]
-        diagonal = SURFACE_TERM + link[0] + link[1] + link[2] + link[3]
-        surface = lev > 0
-        sw[pl.ds(own, BY), :] = jnp.where(surface, 1.0 / jnp.sqrt(diagonal), 0.0)
-        dw[pl.ds(own, BY), :] = jnp.where(surface, diagonal, 0.0)
-        for ref, value in zip((le, lw, ln, ls), link):
-            ref[pl.ds(own, BY), :] = value
-        return 0
-
-    lax.fori_loop(0, blocks, speed_body, 0)
-    def tracer_body(j, _):
+        return carry
+
+    lax.fori_loop(1, blocks - 1, speed_body, 0)
+    wait_recv()
+    for side, row in ((0, PAD - 1), (1, PAD + rows)):
+        for f in range(3):
+            for k in range(tiers):
+                fields[f][k, pl.ds(row, 1), :] = ins_r[side, pl.ds(f * tiers + k, 1), :]
+        levpad[pl.ds(row, 1), :] = ins_r[side, pl.ds(3 * tiers, 1), :]
+
+    def combine(from_west, from_east):
+        return jnp.where(odd, pltpu.roll(from_west, 1, 1), pltpu.roll(from_east, cols - 1, 1))
+
+    lax.fori_loop(0, 2, lambda i, carry: speed_body(i * (blocks - 1), carry), 0)
+
+    lev_own = iew_s[3 * pairs]
+    lev_halo = combine(iew_r[0, 3 * pairs], iew_r[1, 3 * pairs])
+    iew_c[3 * pairs] = lev_halo
+    face = jnp.minimum(lev_own, lev_halo)
+    face = face + pltpu.roll(face, cols // 2, 1)
+    outward = jnp.where(odd, -1.0, 1.0)
+    load = tx_edge = ty_edge = zero
+    for h in range(pairs):
+        own_, halo_ = [], []
+        for f in range(3):
+            own_.append(iew_s[f * pairs + h])
+            halo_.append(combine(iew_r[0, f * pairs + h], iew_r[1, f * pairs + h]))
+        (t, u, v), (th, uh, vh) = own_, halo_
+        weight = jnp.where(high_half, thick[2 * h + 1], thick[2 * h])
+        wet = face > jnp.where(high_half, 2.0 * h + 1.0, 2.0 * h)
+        part = (-0.5 * HEAT_DILATION) * weight * (th - t)
+        other = pltpu.roll(part, cols // 2, 1)
+        slope = load + part + jnp.where(high_half, other, 0.0)
+        load = load + part + other
+        cu = TIME_STEP * jnp.where(wet, VISCOSITY * (uh - u) - outward * slope, 0.0)
+        cv = TIME_STEP * jnp.where(wet, VISCOSITY * (vh - v), 0.0)
+        ct = TIME_STEP * jnp.where(
+            wet, DIFFUSIVITY * (th - t) - outward * (0.25 * (u + uh) * (t + th)), 0.0
+        )
+        iew_c[h] = ct
+        iew_c[pairs + h] = cu
+        iew_c[2 * pairs + h] = cv
+        tx_edge = tx_edge + weight * cu
+        ty_edge = ty_edge + weight * cv
+    tx_edge = tx_edge + pltpu.roll(tx_edge, cols // 2, 1)
+    ty_edge = ty_edge + pltpu.roll(ty_edge, cols // 2, 1)
+    for j in range(blocks):
+        here, shift = pl.ds(BY * j, BY), cols - 1 - 2 * j
+        pad = pl.ds(PAD + BY * j, BY)
+        txs[here, :] = txs[here, :] + jnp.where(edge, pltpu.roll(tx_edge, shift, 1), 0.0)
+        typad[pad, :] = typad[pad, :] + jnp.where(edge, pltpu.roll(ty_edge, shift, 1), 0.0)
+
+    def beside(value, halo):
+        e = jnp.where(last, halo, pltpu.roll(value, cols - 1, 1))
+        w = jnp.where(first, halo, pltpu.roll(value, 1, 1))
+        return e, w
+
+    def coefficients():
+        for j in range(blocks):
+            at, here = PAD + BY * j, pl.ds(BY * j, BY)
+            lev = levpad[pl.ds(at, BY), :]
+            lev_e, lev_w = beside(lev, pltpu.roll(iew_c[3 * pairs], cols - 1 - 2 * j, 1))
+            lev_n = levpad[pl.ds(at + 1, BY), :]
+            lev_s = levpad[pl.ds(at - 1, BY), :]
+            h = depth(lev)
+            surface = lev > 0
+            link = [
+                jnp.where(surface & (o > 0), 0.5 * (h + depth(o)), 0.0)
+                for o in (lev_e, lev_w, lev_n, lev_s)
+            ]
+            diagonal = SURFACE_TERM + link[0] + link[1] + link[2] + link[3]
+            sw[here, :] = jnp.where(surface, 1.0 / jnp.sqrt(diagonal), 0.0)
+            dw[here, :] = jnp.where(surface, diagonal, 0.0)
+            for ref, value in zip((le, lw, ln, ls), link):
+                ref[here, :] = value
+
+    def tracer_body(j, carry):
         at = pl.multiple_of(PAD + BY * j, BY)
         own = pl.multiple_of(BY * j, BY)
-        lev, lev_e, lev_w, lev_n, lev_s = faces(j, at)
-        me, mw, mn, ms = [jnp.minimum(lev, o) for o in (lev_e, lev_w, lev_n, lev_s)]
+        lev, me, mn, ms = inner_faces(at)
         for k in range(tiers):
             t = tpad[k, pl.ds(at, BY), :]
             u = upad[k, pl.ds(at, BY), :]
             v = vpad[k, pl.ds(at, BY), :]
-            te, tw = field_beside(0, k, j, t)
-            ue, uw = field_beside(1, k, j, u)
+            te, ue = east_of(t), east_of(u)
             tn, ts = tpad[k, pl.ds(at + 1, BY), :], tpad[k, pl.ds(at - 1, BY), :]
             vn, vs = vpad[k, pl.ds(at + 1, BY), :], vpad[k, pl.ds(at - 1, BY), :]
+            ge = jnp.where(me > k, DIFFUSIVITY * (te - t) - 0.25 * (u + ue) * (t + te), 0.0)
             flow = (
-                jnp.where(me > k, DIFFUSIVITY * (te - t) - 0.25 * (u + ue) * (t + te), 0.0)
-                + jnp.where(mw > k, DIFFUSIVITY * (tw - t) + 0.25 * (u + uw) * (t + tw), 0.0)
+                (ge - west_of(ge))
                 + jnp.where(mn > k, DIFFUSIVITY * (tn - t) - 0.25 * (v + vn) * (t + tn), 0.0)
                 + jnp.where(ms > k, DIFFUSIVITY * (ts - t) + 0.25 * (v + vs) * (t + ts), 0.0)
             )
-            tnext[k, pl.ds(own, BY), :] = jnp.where(lev > k, t + TIME_STEP * flow, 0.0)
-        return 0
+            shift = cols // 2 - 1 - 2 * j + (0 if k % 2 else cols // 2)
+            ct, cu, cv = [
+                jnp.where(edge, pltpu.roll(iew_c[f * pairs + k // 2], shift, 1), 0.0)
+                for f in range(3)
+            ]
+            here = pl.ds(own, BY)
+            tnext[k, here, :] = jnp.where(lev > k, t + TIME_STEP * flow, 0.0) + ct
+            unext[k, here, :] = unext[k, here, :] + cu
+            vnext[k, here, :] = vnext[k, here, :] + cv
+        return carry
 
     def tracer_part(part, parts):
         lax.fori_loop(part * blocks // parts, (part + 1) * blocks // parts, tracer_body, 0)
@@ -339,7 +391,7 @@
             dst[pad_block(j), :] = y
 
     wait = send_surface(0, lambda j: txs[block(j), :], typad)
-    tracer_part(0, 5)
+    coefficients()
     wait()
     halo = halo_of(0, typad)
     for j in range(blocks):
@@ -375,7 +427,7 @@
             sums[i, k] = dot(at_block(images[i]), at_pad(basis[k]))
         if k:
             sums[k - 1, k - 1] = dot(at_block(images[k - 1]), at_pad(basis[k - 1]))
-        tracer_part(k + 1, ITERS + 1)
+        tracer_part(k, ITERS)
         if k + 1 == ITERS:
             keys = list(sums)
             tiles = [sums[key] for key in keys]

time: 43.5 us -> 41 us (0.943)
  Pallas kernels: 42.7 us -> 40.2 us
    pallas_call x1, Pallas kernels: 39.1 us -> 36.6 us  [local(): pl.pallas_call(functools.partial(kernel, nx, ny, tiers, rows, cols), out_...]
where the time goes in v3:
time: 41 us; the launch traced here: 40.8 us
  Pallas kernels  40.2 us (98%)
  between operations  0.64 us (2%)
    pallas_call x1, Pallas kernels, local(): pl.pallas_call(functools.partial(kernel, nx, ny, tiers, rows, cols), out_...  36.6 us
    pallas_call x1, Pallas kernels, local(): pl.pallas_call(write_kernel, out_shape=shapes, in_specs=[vmem_spec] * 4,...  3.59 us

profile of v3, /device:TPU:0, one launch (start us, length us, event | category | flops | bytes accessed | tf_op | source)
XLA Modules:
  0.0 40.8 jit_solution(7090128935941492442)
XLA Ops:
  0.6 36.6 %ocean_step.1 = (f32[8,256,128]{2,1,0:T(8,128)}, f32[8,256,128]{2,1,0:T(8,128)}, f32[8,256,128]{2,1,0:T(8,128)}, f32[256,128]{1,0:T(8,128)}) custom-call(f32[8,256,128]{2,1,0:T(8,128)} %t_hbm.1, f32[8,256,128]{2,1,0:T(8,128)} %u_hbm.1, f32[8,256,128]{2,1,0:T(8,128)} %v_hbm.1, s32[256,128]{1,0:T(8,128)} %lev_hbm.1, bf16[256,256]{1,0:T(8,128)(2,1)} %constant.2.clone.op_ref), custom_call_target="tpu_custom_call" | custom-call | tf_op jit(solution)/shard_map/ocean_step/pallas_call | solution.py:547
  37.2 3.6 %write_results.1 = (f32[8,256,128]{2,1,0:T(8,128)}, f32[8,256,128]{2,1,0:T(8,128)}, f32[8,256,128]{2,1,0:T(8,128)}, f32[256,128]{1,0:T(8,128)}) custom-call(f32[8,256,128]{2,1,0:T(8,128)} %get-tuple-element.8.refs_0_, f32[8,256,128]{2,1,0:T(8,128)} %get-tuple-element.9.refs_1_, f32[8,256,128]{2,1,0:T(8,128)} %get-tuple-element.10.refs_2_, ...), custom_call_target="tpu_custom_call" | custom-call | tf_op jit(solution)/shard_map/write_results/pallas_call | solution.py:575

commit v4 on v3

--- a/solution.py
+++ b/solution.py
@@ -109,7 +109,7 @@
         out.append(jnp.where(here, a, carry[3 * pairs]))
         return tuple(out)
 
-    packed = lax.fori_loop(0, blocks, pack_body, (zero,) * (3 * pairs + 1))
+    packed = lax.fori_loop(0, blocks, pack_body, (zero,) * (3 * pairs + 1), unroll=8)
     for i, value in enumerate(packed):
         iew_s[i] = value
     for side, row in ((0, PAD + rows - 1), (1, PAD)):
@@ -224,7 +224,7 @@
         typad[pl.ds(at, BY), :] = ty
         return carry
 
-    lax.fori_loop(1, blocks - 1, speed_body, 0)
+    lax.fori_loop(1, blocks - 1, speed_body, 0, unroll=3)
     wait_recv()
     for side, row in ((0, PAD - 1), (1, PAD + rows)):
         for f in range(3):

time: 41 us -> 36.9 us (0.90)
  Pallas kernels: 40.2 us -> 36.1 us
    pallas_call x1, Pallas kernels: 36.6 us -> 32.6 us  [local(): pl.pallas_call(functools.partial(kernel, nx, ny, tiers, rows, cols), out_...]
where the time goes in v4:
time: 36.9 us; the launch traced here: 36.8 us
  Pallas kernels  36.1 us (98%)
  between operations  0.64 us (2%)
    pallas_call x1, Pallas kernels, local(): pl.pallas_call(functools.partial(kernel, nx, ny, tiers, rows, cols), out_...  32.6 us
    pallas_call x1, Pallas kernels, local(): pl.pallas_call(write_kernel, out_shape=shapes, in_specs=[vmem_spec] * 4,...  3.59 us

profile of v4, /device:TPU:0, one launch (start us, length us, event | category | flops | bytes accessed | tf_op | source)
XLA Modules:
  0.0 36.8 jit_solution(5824102783607818720)
XLA Ops:
  0.6 32.6 %ocean_step.1 = (f32[8,256,128]{2,1,0:T(8,128)}, f32[8,256,128]{2,1,0:T(8,128)}, f32[8,256,128]{2,1,0:T(8,128)}, f32[256,128]{1,0:T(8,128)}) custom-call(f32[8,256,128]{2,1,0:T(8,128)} %t_hbm.1, f32[8,256,128]{2,1,0:T(8,128)} %u_hbm.1, f32[8,256,128]{2,1,0:T(8,128)} %v_hbm.1, s32[256,128]{1,0:T(8,128)} %lev_hbm.1, bf16[256,256]{1,0:T(8,128)(2,1)} %constant.2.clone.op_ref), custom_call_target="tpu_custom_call" | custom-call | tf_op jit(solution)/shard_map/ocean_step/pallas_call | solution.py:547
  33.2 3.6 %write_results.1 = (f32[8,256,128]{2,1,0:T(8,128)}, f32[8,256,128]{2,1,0:T(8,128)}, f32[8,256,128]{2,1,0:T(8,128)}, f32[256,128]{1,0:T(8,128)}) custom-call(f32[8,256,128]{2,1,0:T(8,128)} %get-tuple-element.8.refs_0_, f32[8,256,128]{2,1,0:T(8,128)} %get-tuple-element.9.refs_1_, f32[8,256,128]{2,1,0:T(8,128)} %get-tuple-element.10.refs_2_, ...), custom_call_target="tpu_custom_call" | custom-call | tf_op jit(solution)/shard_map/write_results/pallas_call | solution.py:575
